TPU v7x, 32 devices: a whole 2x2x4 slice. The times are simulated.
32 devices in a mesh: dp: 4 (over y, x), mp: 8 (over z, core).
Axes of the slice: x: 2, y: 2, z: 4, core: 2. Of those that a mesh axis runs over, the one named last changes fastest.
Arguments:
- out_grads: bfloat16 [512, 28672], P('dp', 'mp'), may hold values from -6 to 6
- inputs: bfloat16 [512, 8192], P('mp', 'dp'), may hold values from -6 to 6
- out_basis: bfloat16 [28672, 14336], P('mp', 'dp'), may hold values from -0.03125 to 0.03125
- in_basis: bfloat16 [8192, 8192], P('dp', 'mp'), may hold values from -0.0625 to 0.0625
- query_out: bfloat16 [128, 28672], P('dp', 'mp'), may hold values from -2.390625 to 2.390625
- query_in: bfloat16 [128, 8192], P('mp', 'dp'), may hold values from -2.390625 to 2.390625
- damping: float32 [1], replicated, may hold values from 0.5 to 2
Outputs:
- eigenvalues: float32 [14336, 8192], P('dp', 'mp')
- preconditioned: bfloat16 [4, 14336, 8192], P(None, 'dp', 'mp')
All inputs are finite; a program needn't handle non-finite values.
Results may differ from a plain program's by a relative error of at most 0.033.
Values may be sent and summed in bfloat16 or wider, within the bound.
No kernel may reach another device: no remote copies, remote signals or barrier semaphores. Data moves between devices by JAX's collectives and lax.ppermute only.
A program may use at most 128 MiB of HBM per device.

v0:
```python
import jax
import jax.numpy as jnp
from jax import lax
from jax.experimental import pallas as pl
from jax.experimental.pallas import tpu as pltpu
from jax.sharding import PartitionSpec as P

QUARTERS = 4
HALVES = 2
PIECES = QUARTERS * HALVES
MIB = 1 << 20
LANES = 128
CHIP = 2


def tile_of(width, limit):
    return max(t for t in range(LANES, limit + 1, LANES) if width % t == 0)


def contract_rows(left, right):
    return lax.dot_general(
        left, right, (((0,), (0,)), ((), ())), preferred_element_type=jnp.float32
    )


def streams_of(width):
    return max(count for count in (1, 2) if width % (count * LANES) == 0)


def in_hbm(x):
    return pltpu.with_memory_space_constraint(x, pltpu.HBM)


def add_rounded(left, right):
    return (left.astype(jnp.float32) + right.astype(jnp.float32)).astype(left.dtype)


class Order:
    def __init__(self):
        self.token = None

    def call(
        self, kernel, operands, out_shape, in_specs=None, out_specs=None, unread=(),
        vmem=6 * MIB, **options,
    ):
        out_shape = list(out_shape)
        whole = pl.BlockSpec(memory_space=pltpu.VMEM)
        anywhere = pl.BlockSpec(memory_space=pl.ANY)
        in_specs = [whole] * len(operands) if in_specs is None else list(in_specs)
        out_specs = [whole] * len(out_shape) if out_specs is None else list(out_specs)
        given, made = len(operands), len(out_shape)
        tokens = [*unread] if self.token is None else [*unread, self.token]

        def body(*refs):
            start = given + len(tokens)
            kernel(*refs[:given], *refs[start:start + made], *refs[start + made + 1:])

        *results, self.token = pl.pallas_call(
            body,
            in_specs=in_specs + [anywhere] * len(tokens),
            out_specs=out_specs + [anywhere],
            out_shape=out_shape + [jax.ShapeDtypeStruct((8, LANES), jnp.float32)],
            compiler_params=pltpu.CompilerParams(vmem_limit_bytes=vmem),
            **options,
        )(*operands, *tokens)
        return results

    def add(self, *pairs, unread=()):
        count = len(pairs)

        def kernel(*refs):
            for i in range(count):
                refs[2 * count + i][...] = add_rounded(refs[2 * i][...], refs[2 * i + 1][...])

        shapes = [jax.ShapeDtypeStruct(x.shape, x.dtype) for x, _ in pairs]
        operands = [x for pair in pairs for x in pair]
        return self.call(kernel, operands, shapes, unread=unread, name="add")


def swap_quarter(x, bits):
    size = lax.axis_size("dp")
    step = bits * (size // QUARTERS)
    return lax.ppermute(x, "dp", [(i, i ^ step) for i in range(size)])


def swap_core(x):
    size = lax.axis_size("mp")
    return lax.ppermute(x, "mp", [(i, i ^ 1) for i in range(size)])


def move_chip(x, pairs):
    return lax.ppermute(
        x, "mp", [(HALVES * a + c, HALVES * b + c) for a, b in pairs for c in range(HALVES)]
    )


class LineSum:
    def __init__(self, place, count):
        self.place, self.count = place, count
        self.chips = lax.axis_size("mp") // HALVES
        self.deepest = self.chips // 2 - 1
        self.lag = 2 * self.deepest + 1
        self.step, self.own, self.sent, self.came = 0, [], [], None

    def swaps(self, odd):
        found = []
        for chip in range(odd, self.chips - 1, 2):
            depths = [min(c, self.chips - 1 - c) for c in (chip, chip + 1)]
            if depths[0] == depths[1]:
                ages = [depths[0]]
            else:
                ages = [min(depths), self.lag - max(depths)]
            if any(0 <= self.step - age < self.count for age in ages):
                found += [(chip, chip + 1), (chip + 1, chip)]
        return found

    def advance(self, order, chunk, unread=()):
        deepest, chips = self.deepest, self.chips
        keep, other = chunk if chunk is not None else (None, None)
        operands = [self.place]
        own = list(self.own)
        if chunk is not None:
            operands += [keep, other]
        base = len(operands)
        history = (own[::-1] + [own[0] if own else keep] * deepest)[:deepest]
        some = keep if keep is not None else own[-1]
        sent = (self.sent[::-1] + [(some, some)] * max(deepest, 1))[:max(deepest, 1)]
        came = self.came if self.came is not None else (some, some)
        operands += history + [x for pair in sent for x in pair] + list(came)
        smem, whole = pl.BlockSpec(memory_space=pltpu.SMEM), pl.BlockSpec(memory_space=pltpu.VMEM)
        fresh = chunk is not None

        def kernel(*refs):
            place_ref, rest = refs[0], refs[base:]
            past = rest[:deepest]
            sents = rest[deepest:deepest + 2 * len(sent)]
            even, odd = rest[deepest + 2 * len(sent):][:2]
            outs = rest[deepest + 2 * len(sent) + 2:]
            even_ref, odd_ref, total_ref = outs[:3]
            if fresh:
                own_ref = outs[3]
                own_ref[...] = add_rounded(refs[1][...], refs[2][...])
            for chip in range(chips):
                depth, left_side = min(chip, chips - 1 - chip), chip < chips // 2
                by_even = left_side == (chip % 2 == 0)
                outer, inner = (odd, even) if by_even else (even, odd)
                to_inner, to_outer = (even_ref, odd_ref) if by_even else (odd_ref, even_ref)
                side = 0 if by_even else 1

                @pl.when(place_ref[CHIP] == chip)
                def _(depth=depth, outer=outer, inner=inner, to_inner=to_inner,
                      to_outer=to_outer, side=side):
                    if depth == 0:
                        to_inner[...] = own_ref[...] if fresh else inner[...]
                    else:
                        to_inner[...] = add_rounded(past[depth - 1][...], outer[...])
                    if depth == deepest:
                        to_outer[...] = add_rounded(sents[side][...], inner[...])
                    else:
                        to_outer[...] = inner[...]
                    if depth == 0:
                        total_ref[...] = to_outer[...]
                    else:
                        total_ref[...] = sents[2 * (depth - 1) + 1 - side][...]

        shape = jax.ShapeDtypeStruct(some.shape, some.dtype)
        even, odd, total, *mine = order.call(
            kernel, operands, [shape] * (4 if fresh else 3),
            [smem] + [whole] * (len(operands) - 1), unread=unread, name="line_step",
        )
        self.own = (own + (mine if fresh else own[-1:]))[-max(deepest, 1):]
        self.sent = (self.sent + [(even, odd)])[-max(deepest, 1):]
        self.came = tuple(
            move_chip(x, swaps) if swaps else x
            for x, swaps in ((even, self.swaps(0)), (odd, self.swaps(1)))
        )
        ready = self.step >= self.lag
        self.step += 1
        return total if ready else None


def join_rows(order, tokens, queries, act_tokens, act_queries):
    length, rank = tokens.shape[0] // HALVES, queries.shape[0] // HALVES
    act_length = act_tokens.shape[0]

    def kernel(
        tokens_ref, queries_ref, act_tokens_ref, act_queries_ref, low_ref, high_ref, act_ref, sems
    ):
        copies = []
        for h, ref in enumerate((low_ref, high_ref)):
            copies += [
                pltpu.make_async_copy(
                    tokens_ref.at[pl.ds(h * length, length)],
                    ref.at[pl.ds(0, length)],
                    sems.at[h, 0],
                ),
                pltpu.make_async_copy(
                    queries_ref.at[pl.ds(h * rank, rank)],
                    ref.at[pl.ds(length, rank)],
                    sems.at[h, 1],
                ),
            ]
        copies.append(
            pltpu.make_async_copy(
                act_tokens_ref, act_ref.at[pl.ds(0, act_length)], sems.at[HALVES, 0]
            )
        )
        for copy in copies:
            copy.start()
        act_ref[act_length:] = act_queries_ref[...]
        for copy in copies:
            copy.wait()

    half = jax.ShapeDtypeStruct((length + rank, tokens.shape[1]), tokens.dtype)
    act = (act_length + act_queries.shape[0], act_tokens.shape[1])
    anywhere, whole = pl.BlockSpec(memory_space=pl.ANY), pl.BlockSpec(memory_space=pltpu.VMEM)
    return order.call(
        kernel,
        [in_hbm(tokens), in_hbm(queries), in_hbm(act_tokens), in_hbm(act_queries)],
        [half, half, jax.ShapeDtypeStruct(act, act_tokens.dtype)],
        [anywhere, anywhere, anywhere, whole],
        scratch_shapes=[pltpu.SemaphoreType.DMA((HALVES + 1, 2))],
        name="join_rows",
    )


def place_rows(place_ref, low_ref, high_ref, rows_ref):
    half = low_ref.shape[0]
    core = place_ref[1]
    rows_ref[pl.ds(pl.multiple_of(core * half, 16), half), :] = low_ref[...]
    rows_ref[pl.ds(pl.multiple_of((1 - core) * half, 16), half), :] = high_ref[...]


def multiply(order, place, low, high, basis, held, unread=()):
    half, depth = low.shape
    width = basis.shape[1]
    first = held is None

    streams = streams_of(width)
    block = width // streams
    tile = tile_of(width, 512)

    def product(rows_ref, basis_ref, keep_refs, send_refs, at):
        terms = jnp.dot(
            rows_ref[...], basis_ref[:, at:at + tile], preferred_element_type=jnp.float32
        ).astype(rows_ref.dtype)
        for b in range(streams):
            start, stop = max(at, b * block), min(at + tile, (b + 1) * block)
            if start < stop:
                columns = slice(start - b * block, stop - b * block)
                keep_refs[b][:, columns] = terms[:half, start - at:stop - at]
                send_refs[b][:, columns] = terms[half:, start - at:stop - at]

    def load_kernel(place_ref, low_ref, high_ref, basis_ref, *refs):
        keep_refs, send_refs = refs[:streams], refs[streams:2 * streams]
        held_ref, rows_ref, sems = refs[2 * streams:]
        copies = [
            pltpu.make_async_copy(
                basis_ref.at[:, pl.ds(at, tile)],
                held_ref.at[:, pl.ds(at, tile)],
                sems.at[at // tile],
            )
            for at in range(0, width, tile)
        ]
        for copy in copies:
            copy.start()
        place_rows(place_ref, low_ref, high_ref, rows_ref)
        for i, copy in enumerate(copies):
            copy.wait()
            product(rows_ref, held_ref, keep_refs, send_refs, i * tile)

    def held_kernel(place_ref, low_ref, high_ref, held_ref, *refs):
        keep_refs, send_refs, rows_ref = refs[:streams], refs[streams:2 * streams], refs[-1]
        place_rows(place_ref, low_ref, high_ref, rows_ref)
        for at in range(0, width, tile):
            product(rows_ref, held_ref, keep_refs, send_refs, at)

    smem = pl.BlockSpec(memory_space=pltpu.SMEM)
    whole = pl.BlockSpec(memory_space=pltpu.VMEM)
    anywhere = pl.BlockSpec(memory_space=pl.ANY)
    outs = [jax.ShapeDtypeStruct((half, block), low.dtype)] * (2 * streams)
    scratch = [pltpu.VMEM((HALVES * half, depth), low.dtype)]
    if first:
        return order.call(
            load_kernel,
            [place, low, high, basis],
            outs + [pltpu.VMEM(basis.shape, basis.dtype)],
            [smem, whole, whole, anywhere],
            scratch_shapes=scratch + [pltpu.SemaphoreType.DMA((width // tile,))],
            name="load_and_multiply",
        )
    held = pltpu.with_memory_space_constraint(held, pltpu.VMEM)
    return order.call(
        held_kernel,
        [place, low, high, held],
        outs,
        [smem, whole, whole, whole],
        unread=unread,
        scratch_shapes=scratch,
        name="multiply",
    )


def multiply_activations(order, rows, basis, unread=()):
    count, depth = rows.shape
    width, half = basis.shape[1], rows.shape[0] // HALVES
    tile = tile_of(width, 256)

    def kernel(rows_ref, basis_ref, low_ref, high_ref):
        for h, ref in enumerate((low_ref, high_ref)):
            terms = jnp.dot(
                rows_ref[h * half:(h + 1) * half, :],
                basis_ref[...],
                preferred_element_type=jnp.float32,
            )
            ref[...] = terms.astype(ref.dtype)

    out = pl.BlockSpec((half, tile), lambda i: (0, i))
    return order.call(
        kernel,
        [in_hbm(rows), in_hbm(basis)],
        [jax.ShapeDtypeStruct((half, width), rows.dtype)] * HALVES,
        [
            pl.BlockSpec((count, depth), lambda i: (0, 0)),
            pl.BlockSpec((depth, tile), lambda i: (0, i)),
        ],
        [out, out],
        unread=unread,
        grid=(width // tile,),
        name="multiply_activations",
    )


def rotated_places(core):
    return [(0, core), (2 - core, core), (1 + core, core), (3, core)]


def correct_kernel(tokens, place_ref, damping_ref, *refs):
    groups = 2 * QUARTERS
    rot_refs, act_refs = refs[:groups], refs[groups:groups + HALVES]
    eig_ref, pre_ref, rot_tok, rot_qry, act_tok, act_qry = refs[groups + HALVES:]
    queries = rot_refs[0].shape[0] - tokens
    quarter, core = place_ref[0], place_ref[1]

    def put(tok, qry, piece, values):
        tok[pl.ds(pl.multiple_of(piece * tokens, 16), tokens), :] = values[:tokens]
        qry[pl.ds(pl.multiple_of(piece * queries, 16), queries), :] = values[tokens:]

    @pl.when(pl.program_id(0) == 0)
    def _():
        per_ref = PIECES // HALVES
        size = tokens + queries
        for piece in range(PIECES):
            at = piece % per_ref * size
            put(act_tok, act_qry, piece, act_refs[piece // per_ref][at:at + size, :])

    for held, refs_held in ((core, rot_refs[:QUARTERS]), (1 - core, rot_refs[QUARTERS:])):
        for (bits, half), ref in zip(rotated_places(held), refs_held):
            put(rot_tok, rot_qry, (quarter ^ bits) * HALVES + half, ref[...])

    length = tokens * PIECES // 2
    total = None
    for seq in range(2):
        rows = slice(seq * length, (seq + 1) * length)
        rotated = contract_rows(rot_tok[rows, :], act_tok[rows, :])
        square = rotated * rotated
        total = square if total is None else total + square
    eig = total * (1.0 / (2 * length))
    eig_ref[...] = eig
    inverse = 1.0 / (eig + damping_ref[0])
    rank = queries * HALVES
    for query in range(QUARTERS):
        rows = slice(query * rank, (query + 1) * rank)
        product = contract_rows(rot_qry[rows, :], act_qry[rows, :])
        pre_ref[query] = (product * inverse).astype(pre_ref.dtype)


def correct(order, tokens, place, damping, rot, act, block, outs, made):
    size, width = rot[0].shape
    rows, ins = act[0].shape
    queries = size - tokens
    tile = tile_of(width, 256)
    steps = width // tile
    smem = pl.BlockSpec(memory_space=pltpu.SMEM)
    dtype = rot[0].dtype
    operands = [place, damping, *rot, *act]
    count, kept = len(operands), len(made)
    return order.call(
        lambda *refs: correct_kernel(tokens, *refs[:count], *refs[count + kept:]),
        operands + list(made),
        [
            jax.ShapeDtypeStruct((outs, ins), jnp.float32),
            jax.ShapeDtypeStruct((QUARTERS, outs, ins), dtype),
        ],
        [smem, smem]
        + [pl.BlockSpec((size, tile), lambda i: (0, i))] * len(rot)
        + [pl.BlockSpec((rows, ins), lambda i: (0, 0))] * len(act)
        + [pl.BlockSpec(memory_space=pl.ANY)] * kept,
        [
            pl.BlockSpec((tile, ins), lambda i: (block * steps + i, 0)),
            pl.BlockSpec((QUARTERS, tile, ins), lambda i: (0, block * steps + i, 0)),
        ],
        input_output_aliases={count + i: i for i in range(kept)},
        grid=(steps,),
        scratch_shapes=[
            pltpu.VMEM((PIECES * tokens, tile), dtype),
            pltpu.VMEM((PIECES * queries, tile), dtype),
            pltpu.VMEM((PIECES * tokens, ins), dtype),
            pltpu.VMEM((PIECES * queries, ins), dtype),
        ],
        vmem=32 * MIB,
        name="correct",
    )


def outer_rows(tokens, queries):
    size = lax.axis_size("dp")
    index = lax.axis_index("dp")
    step = 1
    while step < size // QUARTERS:
        pairs = [(i, i ^ step) for i in range(size)]
        first = (index // step) % 2 == 0

        def joined(x):
            other = lax.ppermute(x, "dp", pairs)
            return jnp.where(
                first, jnp.concatenate([x, other]), jnp.concatenate([other, x])
            )

        tokens, queries = joined(tokens), joined(queries)
        step *= 2
    return tokens, queries


class QuarterSum:
    def __init__(self, low, high):
        size = lax.axis_size("dp")
        outer = size // QUARTERS
        self.hops = [(outer, 2 * outer), (2 * outer, outer)]
        step = 1
        while step < outer:
            self.hops.append((step, step))
            step *= 2
        self.size, self.pair, self.hop = size, (low, high), 0
        self.send()

    def send(self):
        self.came = [
            lax.ppermute(x, "dp", [(i, i ^ step) for i in range(self.size)])
            for x, step in zip(self.pair, self.hops[self.hop])
        ]

    def add(self, order):
        self.pair = order.add(*zip(self.pair, self.came))
        self.hop += 1
        if self.hop < len(self.hops):
            self.send()


def activation_rows(rows, tokens):
    blocks = lax.all_gather(rows, "mp", axis=0)
    holders, _, width = blocks.shape
    if holders != PIECES:
        blocks = jnp.concatenate(
            [
                blocks[:, :tokens].reshape(PIECES, -1, width),
                blocks[:, tokens:].reshape(PIECES, -1, width),
            ],
            axis=1,
        )
    return blocks.reshape(-1, width)


def shards(out_grads, inputs, out_basis, in_basis, query_out, query_in, damping):
    order = Order()
    dp, mp = lax.axis_index("dp"), lax.axis_index("mp")
    place = jnp.stack(
        [dp // (lax.axis_size("dp") // QUARTERS), mp % HALVES, mp // HALVES]
    ).astype(jnp.int32)

    tokens, queries = outer_rows(out_grads, query_out)
    length = tokens.shape[0] // HALVES
    low, high, act_rows = join_rows(order, tokens, queries, inputs, query_in)
    beside = [swap_quarter(low, 2), swap_quarter(high, 1)]
    behind = [swap_quarter(low, 1), swap_quarter(high, 2)]
    across = [swap_quarter(beside[0], 1), swap_quarter(beside[1], 2)]
    act_rows = activation_rows(act_rows, inputs.shape[0])

    width = out_basis.shape[1]
    lines = [LineSum(place, QUARTERS) for _ in range(streams_of(width))]
    held, acts = None, None
    chunks, late = [], []
    totals, swapped = [[] for _ in lines], [[] for _ in lines]

    def rotate(pair, unread=()):
        nonlocal held
        results = multiply(order, place, *pair, out_basis, held, unread)
        held = results.pop() if held is None else held
        came = [swap_core(x) for x in results[len(lines):]]
        chunks.append(list(zip(results, came)))

    def advance(s, unread=()):
        if s >= len(lines):
            return
        line, pins = lines[s], [*unread, *late]
        late.clear()
        chunk = chunks[line.step][s] if line.step < QUARTERS else None
        total = line.advance(order, chunk, pins)
        if total is not None:
            totals[s].append(total)
            swapped[s].append(swap_core(total))
            late.append(swapped[s][-1])

    def activate(unread=()):
        nonlocal acts
        acts = QuarterSum(*multiply_activations(order, act_rows, in_basis, unread))

    rotate((low, high))
    advance(0)
    advance(1)
    rotate(beside)
    advance(0)
    rotate(behind, [*behind])
    advance(1)
    rotate(across, [*across])
    advance(0)
    advance(1)
    activate()
    advance(0)
    advance(1)
    advance(0)
    acts.add(order)
    advance(1)
    advance(0)
    acts.add(order)
    advance(1)
    advance(0)
    advance(1)
    while acts.hop < len(acts.hops):
        acts.add(order)
    while len(totals[-1]) < QUARTERS:
        for s in range(len(lines)):
            advance(s)

    made = ()
    for s in range(len(lines)):
        rot = totals[s] + swapped[s]
        made = correct(order, length, place, damping, rot, acts.pair, s, width, made)
    return tuple(made)


def solution(mesh):
    placed = (
        P("dp", "mp"),
        P("mp", "dp"),
        P("mp", "dp"),
        P("dp", "mp"),
        P("dp", "mp"),
        P("mp", "dp"),
        P(),
    )
    return jax.shard_map(
        shards,
        mesh=mesh,
        in_specs=placed,
        out_specs=(P("dp", "mp"), P(None, "dp", "mp")),
        check_vma=False,
    )
```

profile of v0, /device:TPU:1, one launch (start us, length us, event | category | flops | bytes accessed | tf_op | source)
XLA Modules:
  0.0 173.4 jit_solution(1839292024448807686)
XLA Ops:
  7.2 2.9 %join_rows.1 = (bf16[80,3584]{1,0:T(8,128)(2,1)S(1)}, bf16[80,3584]{1,0:T(8,128)(2,1)S(1)}, bf16[80,2048]{1,0:T(8,128)(2,1)}, f32[8,128]{1,0:T(8,128)S(1)}) custom-call(bf16[128,3584]{1,0:T(8,128)(2,1)} %refs_0_.1, bf16[32,3584]{1,0:T(8,128)(2,1)} %refs_1_.4, bf16[64,2048]{1,0:T(8,128)(2,1)} %refs_2_.1, bf16[16,2048]{1,0:T(8,128)(2,1)} %refs_3_.2), custom_call_target="tpu_custom_call" | custom-call | tf_op jit(solution)/shard_map/join_rows/pallas_call | solution.py:58
  10.2 2.1 %collective-permute-start = (bf16[80,3584]{1,0:T(8,128)(2,1)S(1)}, bf16[80,3584]{1,0:T(8,128)(2,1)S(1)}, u32[]{:S(2)}, u32[]{:S(2)}) collective-permute-start(bf16[80,3584]{1,0:T(8,128)(2,1)S(1)} %get-tuple-element.95.refs_1_), channel_id=1, source_target_pairs={{0,16},{8,24},{16,0},{24,8},{1,17},{9,25},{17,1},{25,9},{2,18},{10... | collective-permute-start | bytes 1720328 | tf_op jit(solution)/shard_map/ppermute | solution.py:83
  12.3 1.2 collective-permute-start.2
  13.9 10.3 %load_and_multiply.1 = (bf16[80,1792]{1,0:T(8,128)(2,1)S(1)}, bf16[80,1792]{1,0:T(8,128)(2,1)S(1)}, bf16[80,1792]{1,0:T(8,128)(2,1)S(1)}, bf16[80,1792]{1,0:T(8,...) custom-call(s32[3]{0:T(128)S(1)} %pad_add_fusion.refs_0_, ...), custom_call_target="tpu_custom_call" | custom-call | tf_op jit(solution)/shard_map/load_and_multiply/pallas_call | solution.py:58
  24.2 1.6 collective-permute-start.5
  25.8 1.2 collective-permute-done.5.refs_2_
  27.0 1.4 line_step.14
  28.4 1.7 collective-permute-start.11
  30.1 1.4 line_step.15
  31.4 5.0 %multiply.3 = (bf16[80,1792]{1,0:T(8,128)(2,1)S(1)}, bf16[80,1792]{1,0:T(8,128)(2,1)S(1)}, bf16[80,1792]{1,0:T(8,128)(2,1)S(1)}, bf16[80,1792]{1,0:T(8,128)(2,1)S(1)}, f32[8,128]{1,0:T(8,128)S(1)}) custom-call(s32[3]{0:T(128)S(1)} %pad_add_fusion.refs_0_, bf16[80,3584]{1,0:T(8,128)(2,1)S(1)} %collective-permute-done.refs_1_, ...), custom_call_target="tpu_custom_call" | custom-call | tf_op jit(solution)/shard_map/multiply/pallas_call | solution.py:58
  36.4 1.0 collective-permute-start.10
  37.4 1.2 collective-permute-start.1
  38.6 1.1 collective-permute-start.3
  39.8 10.5 %collective-permute-done.11.refs_6_ = bf16[80,1792]{1,0:T(8,128)(2,1)S(1)} collective-permute-done((bf16[80,1792]{1,0:T(8,128)(2,1)S(1)}, bf16[80,1792]{1,0:T(8,128)(2,1)S(1)}, u32[]{:S(2)}, u32[]{:S(2)}) %collective-permute-start.11) | collective-permute-done | bytes 286752 | tf_op jit(solution)/shard_map/ppermute | solution.py:92
  50.6 1.6 line_step.16
  52.1 5.0 %multiply.4 = (bf16[80,1792]{1,0:T(8,128)(2,1)S(1)}, bf16[80,1792]{1,0:T(8,128)(2,1)S(1)}, bf16[80,1792]{1,0:T(8,128)(2,1)S(1)}, bf16[80,1792]{1,0:T(8,128)(2,1)S(1)}, f32[8,128]{1,0:T(8,128)S(1)}) custom-call(s32[3]{0:T(128)S(1)} %pad_add_fusion.refs_0_, bf16[80,3584]{1,0:T(8,128)(2,1)S(1)} %collective-permute-done.8.refs_1_.refs_4_, ...), custom_call_target="tpu_custom_call" | custom-call | tf_op jit(solution)/shard_map/multiply/pallas_call | solution.py:58
  57.4 1.0 collective-permute-done.7.refs_6_
  58.3 0.7 collective-permute-start.17
  59.1 0.7 collective-permute-start.18
  59.8 0.8 collective-permute-start.13
  60.6 1.4 line_step.17
  62.0 4.1 %collective-permute-start.14 = (bf16[80,1792]{1,0:T(8,128)(2,1)S(1)}, bf16[80,1792]{1,0:T(8,128)(2,1)S(1)}, u32[]{:S(2)}, u32[]{:S(2)}) collective-permute-start(bf16[80,1792]{1,0:T(8,128)(2,1)S(1)} %get-tuple-element.125.refs_4_), channel_id=1, source_target_pairs={{0,2},{1,3},{2,0},{3,1},{4,6},{5,7},{6,4},{7,5},{8,10},{9,11},{10,... | collective-permute-start | bytes 860168 | tf_op jit(solution)/shard_map/ppermute | solution.py:92
  66.1 0.7 collective-permute-start.15
  66.8 5.7 %multiply.5 = (bf16[80,1792]{1,0:T(8,128)(2,1)S(1)}, bf16[80,1792]{1,0:T(8,128)(2,1)S(1)}, bf16[80,1792]{1,0:T(8,128)(2,1)}, bf16[80,1792]{1,0:T(8,128)(2,1)}, f32[8,128]{1,0:T(8,128)S(1)}) custom-call(s32[3]{0:T(128)S(1)} %pad_add_fusion.refs_0_, bf16[80,3584]{1,0:T(8,128)(2,1)S(1)} %collective-permute-done.1.refs_1_.refs_4_, ...), custom_call_target="tpu_custom_call" | custom-call | tf_op jit(solution)/shard_map/multiply/pallas_call | solution.py:58
  72.5 1.4 line_step.18
  73.9 1.7 collective-permute-start.22
  75.5 0.7 collective-permute-start.23
  77.0 1.4 line_step.19
  78.4 2.4 %collective-permute-start.19 = (bf16[80,1792]{1,0:T(8,128)(2,1)S(1)}, bf16[80,1792]{1,0:T(8,128)(2,1)S(1)}, u32[]{:S(2)}, u32[]{:S(2)}) collective-permute-start(bf16[80,1792]{1,0:T(8,128)(2,1)S(1)} %get-tuple-element.135.refs_4_), channel_id=1, source_target_pairs={{0,2},{1,3},{2,0},{3,1},{4,6},{5,7},{6,4},{7,5},{8,10},{9,11},{10,... | collective-permute-start | bytes 860168 | tf_op jit(solution)/shard_map/ppermute | solution.py:92
  80.8 6.1 %multiply_activations.1 = (bf16[320,1024]{1,0:T(8,128)(2,1)S(1)}, bf16[320,1024]{1,0:T(8,128)(2,1)S(1)}, f32[8,128]{1,0:T(8,128)S(1)}) custom-call(bf16[640,2048]{1,0:T(8,128)(2,1)} %all-gather.3.cloned.1.call-done.refs_0_, bf16[2048,1024]{1,0:T(8,128)(2,1)} %refs_1_.5, f32[8,128]{1,0:T(8,128)S(1)} %get-tuple-element.143.refs_2_), custom_call_target="tpu_custom_call" | custom-call | tf_op jit(solution)/shard_map/multiply_activations/pallas_call | solution.py:58
  86.9 0.7 collective-permute-start.20
  87.6 1.1 line_step.20
  88.7 0.8 collective-permute-start.24
  89.5 1.2 collective-permute-start.31
  90.6 1.3 collective-permute-start.32
  91.9 1.7 collective-permute-start.27
  93.6 0.7 collective-permute-start.28
  94.3 0.7 line_step.21
  95.0 1.0 collective-permute-start.29
  96.0 4.2 %collective-permute-done.27.refs_4_ = bf16[80,1792]{1,0:T(8,128)(2,1)S(1)} collective-permute-done((bf16[80,1792]{1,0:T(8,128)(2,1)S(1)}, bf16[80,1792]{1,0:T(8,128)(2,1)S(1)}, u32[]{:S(2)}, u32[]{:S(2)}) %collective-permute-start.27) | collective-permute-done | bytes 286752 | tf_op jit(solution)/shard_map/ppermute | solution.py:92
  100.2 1.2 collective-permute-start.25
  101.5 0.7 collective-permute-start.26
  102.2 0.8 line_step.22
  103.0 1.8 %collective-permute-start.30 = (bf16[80,1792]{1,0:T(8,128)(2,1)S(1)}, bf16[80,1792]{1,0:T(8,128)(2,1)S(1)}, u32[]{:S(2)}, u32[]{:S(2)}) collective-permute-start(bf16[80,1792]{1,0:T(8,128)(2,1)S(1)} %get-tuple-element.155.refs_3_), channel_id=1, source_target_pairs={{0,1},{1,0},{2,3},{3,2},{4,5},{5,4},{6,7},{7,6},{8,9},{9,8},{10,11... | collective-permute-start | bytes 860168 | tf_op jit(solution)/shard_map/ppermute | solution.py:88
  104.8 1.0 collective-permute-done.31.refs_1_
  105.8 0.8 collective-permute-done.32.refs_3_
  106.9 1.3 collective-permute-start.39
  108.6 5.7 %collective-permute-start.35 = (bf16[80,1792]{1,0:T(8,128)(2,1)S(1)}, bf16[80,1792]{1,0:T(8,128)(2,1)S(1)}, u32[]{:S(2)}, u32[]{:S(2)}) collective-permute-start(bf16[80,1792]{1,0:T(8,128)(2,1)S(1)} %get-tuple-element.163.refs_2_), channel_id=1, source_target_pairs={{0,2},{1,3},{2,0},{3,1},{4,6},{5,7},{6,4},{7,5},{8,10},{9,11},{10,... | collective-permute-start | bytes 860168 | tf_op jit(solution)/shard_map/ppermute | solution.py:92
  114.3 0.7 collective-permute-start.36
  115.6 0.9 collective-permute-start.37
  116.6 4.4 %collective-permute-done.35.refs_4_ = bf16[80,1792]{1,0:T(8,128)(2,1)S(1)} collective-permute-done((bf16[80,1792]{1,0:T(8,128)(2,1)S(1)}, bf16[80,1792]{1,0:T(8,128)(2,1)S(1)}, u32[]{:S(2)}, u32[]{:S(2)}) %collective-permute-start.35) | collective-permute-done | bytes 286752 | tf_op jit(solution)/shard_map/ppermute | solution.py:92
  121.0 1.1 collective-permute-start.33
  122.1 0.7 collective-permute-start.34
  123.4 1.8 %collective-permute-start.38 = (bf16[80,1792]{1,0:T(8,128)(2,1)S(1)}, bf16[80,1792]{1,0:T(8,128)(2,1)S(1)}, u32[]{:S(2)}, u32[]{:S(2)}) collective-permute-start(bf16[80,1792]{1,0:T(8,128)(2,1)S(1)} %get-tuple-element.166.refs_4_), channel_id=1, source_target_pairs={{0,1},{1,0},{2,3},{3,2},{4,5},{5,4},{6,7},{7,6},{8,9},{9,8},{10,11... | collective-permute-start | bytes 860168 | tf_op jit(solution)/shard_map/ppermute | solution.py:88
  125.2 4.3 %collective-permute-start.42 = (bf16[80,1792]{1,0:T(8,128)(2,1)S(1)}, bf16[80,1792]{1,0:T(8,128)(2,1)S(1)}, u32[]{:S(2)}, u32[]{:S(2)}) collective-permute-start(bf16[80,1792]{1,0:T(8,128)(2,1)S(1)} %get-tuple-element.174.refs_2_), channel_id=1, source_target_pairs={{0,2},{1,3},{2,0},{3,1},{4,6},{5,7},{6,4},{7,5},{8,10},{9,11},{10,... | collective-permute-start | bytes 860168 | tf_op jit(solution)/shard_map/ppermute | solution.py:92
  131.0 3.8 %collective-permute-start.41 = (bf16[80,1792]{1,0:T(8,128)(2,1)S(1)}, bf16[80,1792]{1,0:T(8,128)(2,1)S(1)}, u32[]{:S(2)}, u32[]{:S(2)}) collective-permute-start(bf16[80,1792]{1,0:T(8,128)(2,1)S(1)} %get-tuple-element.172.refs_2_), channel_id=1, source_target_pairs={{0,2},{1,3},{2,0},{3,1},{4,6},{5,7},{6,4},{7,5},{8,10},{9,11},{10,... | collective-permute-start | bytes 860168 | tf_op jit(solution)/shard_map/ppermute | solution.py:92
  134.8 1.9 %collective-permute-done.42.refs_4_ = bf16[80,1792]{1,0:T(8,128)(2,1)S(1)} collective-permute-done((bf16[80,1792]{1,0:T(8,128)(2,1)S(1)}, bf16[80,1792]{1,0:T(8,128)(2,1)S(1)}, u32[]{:S(2)}, u32[]{:S(2)}) %collective-permute-start.42) | collective-permute-done | bytes 286752 | tf_op jit(solution)/shard_map/ppermute | solution.py:92
  136.7 1.4 line_step.26
  138.1 0.9 collective-permute-start.44
  139.0 3.8 %collective-permute-done.41.refs_4_ = bf16[80,1792]{1,0:T(8,128)(2,1)S(1)} collective-permute-done((bf16[80,1792]{1,0:T(8,128)(2,1)S(1)}, bf16[80,1792]{1,0:T(8,128)(2,1)S(1)}, u32[]{:S(2)}, u32[]{:S(2)}) %collective-permute-start.41) | collective-permute-done | bytes 286752 | tf_op jit(solution)/shard_map/ppermute | solution.py:92
  142.8 1.4 line_step.27
  144.3 0.7 collective-permute-start.45
  145.6 10.5 %correct.2 = (f32[3584,1024]{1,0:T(8,128)}, bf16[4,3584,1024]{2,1,0:T(8,128)(2,1)}, f32[8,128]{1,0:T(8,128)S(1)}) custom-call(s32[3]{0:T(128)S(1)} %pad_add_fusion.refs_0_, f32[1]{0:T(128)S(6)} %copy.13.refs_1_, bf16[80,1792]{1,0:T(8,128)(2,1)S(1)} %get-tuple-element.145.refs_2_, bf16[80,1792]{1,0:T(8,128)(2,1)S(1)} %get-tuple-element.155.refs_3_, ...), custom_call_target="tpu_custom_call" | custom-call | tf_op jit(solution)/shard_map/correct/pallas_call | solution.py:58
  156.1 10.5 %correct.3 = (f32[3584,1024]{1,0:T(8,128)}, bf16[4,3584,1024]{2,1,0:T(8,128)(2,1)}, f32[8,128]{1,0:T(8,128)}) custom-call(s32[3]{0:T(128)S(1)} %pad_add_fusion.refs_0_, f32[1]{0:T(128)S(6)} %copy.13.refs_1_, bf16[80,1792]{1,0:T(8,128)(2,1)S(1)} %get-tuple-element.147.refs_2_, ...), custom_call_target="tpu_custom_call", output_to_operand_aliasing={{0}: (12, {}), {1}: (13, {})} | custom-call | tf_op jit(solution)/shard_map/correct/pallas_call | solution.py:58
  (56 shorter events, 5.1 us)
Async XLA Ops:
  7.2 73.6 %all-gather.3.cloned.1.call-start = ((), (), s32[]{:S(2)}) async-start(), calls=%async_computation | async-start | bytes 2949120 | tf_op jit(solution)/shard_map/all_gather | solution.py:461
  10.2 21.3 %collective-permute-start = (bf16[80,3584]{1,0:T(8,128)(2,1)S(1)}, bf16[80,3584]{1,0:T(8,128)(2,1)S(1)}, u32[]{:S(2)}, u32[]{:S(2)}) collective-permute-start(bf16[80,3584]{1,0:T(8,128)(2,1)S(1)} %get-tuple-element.95.refs_1_), channel_id=1, source_target_pairs={{0,16},{8,24},{16,0},{24,8},{1,17},{9,25},{17,1},{25,9},{2,18},{10... | collective-permute-start | bytes 1720328 | tf_op jit(solution)/shard_map/ppermute | solution.py:83
  12.3 19.1 %collective-permute-start.2 = (bf16[80,3584]{1,0:T(8,128)(2,1)S(1)}, bf16[80,3584]{1,0:T(8,128)(2,1)S(1)}, u32[]{:S(2)}, u32[]{:S(2)}) collective-permute-start(bf16[80,3584]{1,0:T(8,128)(2,1)S(1)} %get-tuple-element.96.refs_2_), channel_id=1, source_target_pairs={{0,8},{8,0},{16,24},{24,16},{1,9},{9,1},{17,25},{25,17},{2,10},{10... | collective-permute-start | bytes 1720328 | tf_op jit(solution)/shard_map/ppermute | solution.py:83
  13.5 25.1 %collective-permute-start.8 = (bf16[80,3584]{1,0:T(8,128)(2,1)S(1)}, bf16[80,3584]{1,0:T(8,128)(2,1)S(1)}, u32[]{:S(2)}, u32[]{:S(2)}) collective-permute-start(bf16[80,3584]{1,0:T(8,128)(2,1)S(1)} %get-tuple-element.95.refs_1_), channel_id=1, source_target_pairs={{0,8},{8,0},{16,24},{24,16},{1,9},{9,1},{17,25},{25,17},{2,10},{10... | collective-permute-start | bytes 1720328 | tf_op jit(solution)/shard_map/ppermute | solution.py:83
  24.2 2.8 %collective-permute-start.5 = (bf16[80,1792]{1,0:T(8,128)(2,1)S(1)}, bf16[80,1792]{1,0:T(8,128)(2,1)S(1)}, u32[]{:S(2)}, u32[]{:S(2)}) collective-permute-start(bf16[80,1792]{1,0:T(8,128)(2,1)S(1)} %get-tuple-element.102), channel_id=1, source_target_pairs={{0,1},{1,0},{2,3},{3,2},{4,5},{5,4},{6,7},{7,6},{8,9},{9,8},{10,11... | collective-permute-start | bytes 860168 | tf_op jit(solution)/shard_map/ppermute | solution.py:88
  25.7 2.7 %collective-permute-start.4 = (bf16[80,1792]{1,0:T(8,128)(2,1)S(1)}, bf16[80,1792]{1,0:T(8,128)(2,1)S(1)}, u32[]{:S(2)}, u32[]{:S(2)}) collective-permute-start(bf16[80,1792]{1,0:T(8,128)(2,1)S(1)} %get-tuple-element.100), channel_id=1, source_target_pairs={{0,1},{1,0},{2,3},{3,2},{4,5},{5,4},{6,7},{7,6},{8,9},{9,8},{10,11... | collective-permute-start | bytes 860168 | tf_op jit(solution)/shard_map/ppermute | solution.py:88
  27.0 25.1 %collective-permute-start.9 = (bf16[80,3584]{1,0:T(8,128)(2,1)S(1)}, bf16[80,3584]{1,0:T(8,128)(2,1)S(1)}, u32[]{:S(2)}, u32[]{:S(2)}) collective-permute-start(bf16[80,3584]{1,0:T(8,128)(2,1)S(1)} %get-tuple-element.96.refs_2_), channel_id=1, source_target_pairs={{0,16},{8,24},{16,0},{24,8},{1,17},{9,25},{17,1},{25,9},{2,18},{10... | collective-permute-start | bytes 1720328 | tf_op jit(solution)/shard_map/ppermute | solution.py:83
  28.4 21.8 %collective-permute-start.11 = (bf16[80,1792]{1,0:T(8,128)(2,1)S(1)}, bf16[80,1792]{1,0:T(8,128)(2,1)S(1)}, u32[]{:S(2)}, u32[]{:S(2)}) collective-permute-start(bf16[80,1792]{1,0:T(8,128)(2,1)S(1)} %get-tuple-element.114.refs_4_), channel_id=1, source_target_pairs={{0,2},{1,3},{2,0},{3,1},{4,6},{5,7},{6,4},{7,5},{8,10},{9,11},{10,... | collective-permute-start | bytes 860168 | tf_op jit(solution)/shard_map/ppermute | solution.py:92
  36.4 13.8 %collective-permute-start.10 = (bf16[80,1792]{1,0:T(8,128)(2,1)S(1)}, bf16[80,1792]{1,0:T(8,128)(2,1)S(1)}, u32[]{:S(2)}, u32[]{:S(2)}) collective-permute-start(bf16[80,1792]{1,0:T(8,128)(2,1)S(1)} %get-tuple-element.112), channel_id=1, source_target_pairs={{0,1},{1,0},{2,3},{3,2},{4,5},{5,4},{6,7},{7,6},{8,9},{9,8},{10,11... | collective-permute-start | bytes 860168 | tf_op jit(solution)/shard_map/ppermute | solution.py:88
  37.4 22.4 %collective-permute-start.1 = (bf16[80,3584]{1,0:T(8,128)(2,1)S(1)}, bf16[80,3584]{1,0:T(8,128)(2,1)S(1)}, u32[]{:S(2)}, u32[]{:S(2)}) collective-permute-start(bf16[80,3584]{1,0:T(8,128)(2,1)S(1)} %collective-permute-done.refs_1_), channel_id=1, source_target_pairs={{0,8},{8,0},{16,24},{24,16},{1,9},{9,1},{17,25},{25,17},{2,10},{10... | collective-permute-start | bytes 1720328 | tf_op jit(solution)/shard_map/ppermute | solution.py:83
  38.6 23.3 %collective-permute-start.3 = (bf16[80,3584]{1,0:T(8,128)(2,1)S(1)}, bf16[80,3584]{1,0:T(8,128)(2,1)S(1)}, u32[]{:S(2)}, u32[]{:S(2)}) collective-permute-start(bf16[80,3584]{1,0:T(8,128)(2,1)S(1)} %collective-permute-done.2.refs_2_), channel_id=1, source_target_pairs={{0,16},{8,24},{16,0},{24,8},{1,17},{9,25},{17,1},{25,9},{2,18},{10... | collective-permute-start | bytes 1720328 | tf_op jit(solution)/shard_map/ppermute | solution.py:83
  50.2 8.1 %collective-permute-start.7 = (bf16[80,1792]{1,0:T(8,128)(2,1)S(1)}, bf16[80,1792]{1,0:T(8,128)(2,1)S(1)}, u32[]{:S(2)}, u32[]{:S(2)}) collective-permute-start(bf16[80,1792]{1,0:T(8,128)(2,1)S(1)} %get-tuple-element.109.refs_4_), channel_id=1, source_target_pairs={{0,2},{1,3},{2,0},{3,1},{4,6},{5,7},{6,4},{7,5},{8,10},{9,11},{10,... | collective-permute-start | bytes 860168 | tf_op jit(solution)/shard_map/ppermute | solution.py:92
  50.2 8.8 %collective-permute-start.6 = (bf16[80,1792]{1,0:T(8,128)(2,1)S(1)}, bf16[80,1792]{1,0:T(8,128)(2,1)S(1)}, u32[]{:S(2)}, u32[]{:S(2)}) collective-permute-start(bf16[80,1792]{1,0:T(8,128)(2,1)S(1)} %get-tuple-element.107), channel_id=1, source_target_pairs={{0,1},{1,0},{2,3},{3,2},{4,5},{5,4},{6,7},{7,6},{8,9},{9,8},{10,11... | collective-permute-start | bytes 860168 | tf_op jit(solution)/shard_map/ppermute | solution.py:88
  57.1 9.0 %collective-permute-start.16 = (bf16[80,1792]{1,0:T(8,128)(2,1)S(1)}, bf16[80,1792]{1,0:T(8,128)(2,1)S(1)}, u32[]{:S(2)}, u32[]{:S(2)}) collective-permute-start(bf16[80,1792]{1,0:T(8,128)(2,1)S(1)} %get-tuple-element.128), channel_id=1, source_target_pairs={{0,1},{1,0},{2,3},{3,2},{4,5},{5,4},{6,7},{7,6},{8,9},{9,8},{10,11... | collective-permute-start | bytes 860168 | tf_op jit(solution)/shard_map/ppermute | solution.py:88
  58.3 14.1 %collective-permute-start.17 = (bf16[80,1792]{1,0:T(8,128)(2,1)S(1)}, bf16[80,1792]{1,0:T(8,128)(2,1)S(1)}, u32[]{:S(2)}, u32[]{:S(2)}) collective-permute-start(bf16[80,1792]{1,0:T(8,128)(2,1)S(1)} %get-tuple-element.130.refs_4_), channel_id=1, source_target_pairs={{0,2},{1,3},{2,0},{3,1},{4,6},{5,7},{6,4},{7,5},{8,10},{9,11},{10,... | collective-permute-start | bytes 860168 | tf_op jit(solution)/shard_map/ppermute | solution.py:92
  59.1 13.4 %collective-permute-start.18 = (bf16[80,1792]{1,0:T(8,128)(2,1)S(1)}, bf16[80,1792]{1,0:T(8,128)(2,1)S(1)}, u32[]{:S(2)}, u32[]{:S(2)}) collective-permute-start(bf16[80,1792]{1,0:T(8,128)(2,1)S(1)} %get-tuple-element.131.refs_5_), channel_id=1, source_target_pairs={{2,4},{3,5},{4,2},{5,3},{10,12},{11,13},{12,10},{13,11},{18,20},{1... | collective-permute-start | bytes 860168 | tf_op jit(solution)/shard_map/ppermute | solution.py:92
  59.8 16.4 %collective-permute-start.13 = (bf16[80,1792]{1,0:T(8,128)(2,1)S(1)}, bf16[80,1792]{1,0:T(8,128)(2,1)S(1)}, u32[]{:S(2)}, u32[]{:S(2)}) collective-permute-start(bf16[80,1792]{1,0:T(8,128)(2,1)S(1)} %get-tuple-element.123), channel_id=1, source_target_pairs={{0,1},{1,0},{2,3},{3,2},{4,5},{5,4},{6,7},{7,6},{8,9},{9,8},{10,11... | collective-permute-start | bytes 860168 | tf_op jit(solution)/shard_map/ppermute | solution.py:88
  62.0 14.9 %collective-permute-start.14 = (bf16[80,1792]{1,0:T(8,128)(2,1)S(1)}, bf16[80,1792]{1,0:T(8,128)(2,1)S(1)}, u32[]{:S(2)}, u32[]{:S(2)}) collective-permute-start(bf16[80,1792]{1,0:T(8,128)(2,1)S(1)} %get-tuple-element.125.refs_4_), channel_id=1, source_target_pairs={{0,2},{1,3},{2,0},{3,1},{4,6},{5,7},{6,4},{7,5},{8,10},{9,11},{10,... | collective-permute-start | bytes 860168 | tf_op jit(solution)/shard_map/ppermute | solution.py:92
  66.1 10.9 %collective-permute-start.15 = (bf16[80,1792]{1,0:T(8,128)(2,1)S(1)}, bf16[80,1792]{1,0:T(8,128)(2,1)S(1)}, u32[]{:S(2)}, u32[]{:S(2)}) collective-permute-start(bf16[80,1792]{1,0:T(8,128)(2,1)S(1)} %get-tuple-element.126.refs_5_), channel_id=1, source_target_pairs={{2,4},{3,5},{4,2},{5,3},{10,12},{11,13},{12,10},{13,11},{18,20},{1... | collective-permute-start | bytes 860168 | tf_op jit(solution)/shard_map/ppermute | solution.py:92
  73.9 13.0 %collective-permute-start.22 = (bf16[80,1792]{1,0:T(8,128)(2,1)S(1)}, bf16[80,1792]{1,0:T(8,128)(2,1)S(1)}, u32[]{:S(2)}, u32[]{:S(2)}) collective-permute-start(bf16[80,1792]{1,0:T(8,128)(2,1)S(1)} %get-tuple-element.140.refs_4_), channel_id=1, source_target_pairs={{0,2},{1,3},{2,0},{3,1},{4,6},{5,7},{6,4},{7,5},{8,10},{9,11},{10,... | collective-permute-start | bytes 860168 | tf_op jit(solution)/shard_map/ppermute | solution.py:92
  75.5 12.0 %collective-permute-start.23 = (bf16[80,1792]{1,0:T(8,128)(2,1)S(1)}, bf16[80,1792]{1,0:T(8,128)(2,1)S(1)}, u32[]{:S(2)}, u32[]{:S(2)}) collective-permute-start(bf16[80,1792]{1,0:T(8,128)(2,1)S(1)} %get-tuple-element.141.refs_5_), channel_id=1, source_target_pairs={{2,4},{3,5},{4,2},{5,3},{10,12},{11,13},{12,10},{13,11},{18,20},{1... | collective-permute-start | bytes 860168 | tf_op jit(solution)/shard_map/ppermute | solution.py:92
  76.2 11.3 %collective-permute-start.21 = (bf16[80,1792]{1,0:T(8,128)(2,1)}, bf16[80,1792]{1,0:T(8,128)(2,1)}, u32[]{:S(2)}, u32[]{:S(2)}) collective-permute-start(bf16[80,1792]{1,0:T(8,128)(2,1)} %get-tuple-element.138), channel_id=1, source_target_pairs={{0,1},{1,0},{2,3},{3,2},{4,5},{5,4},{6,7},{7,6},{8,9},{9,8},{10,11... | collective-permute-start | bytes 860168 | tf_op jit(solution)/shard_map/ppermute | solution.py:88
  76.9 13.7 %collective-permute-start.12 = (bf16[80,1792]{1,0:T(8,128)(2,1)}, bf16[80,1792]{1,0:T(8,128)(2,1)S(1)}, u32[]{:S(2)}, u32[]{:S(2)}) collective-permute-start(bf16[80,1792]{1,0:T(8,128)(2,1)} %get-tuple-element.121), channel_id=1, source_target_pairs={{0,1},{1,0},{2,3},{3,2},{4,5},{5,4},{6,7},{7,6},{8,9},{9,8},{10,11... | collective-permute-start | bytes 860168 | tf_op jit(solution)/shard_map/ppermute | solution.py:88
  78.4 13.5 %collective-permute-start.19 = (bf16[80,1792]{1,0:T(8,128)(2,1)S(1)}, bf16[80,1792]{1,0:T(8,128)(2,1)S(1)}, u32[]{:S(2)}, u32[]{:S(2)}) collective-permute-start(bf16[80,1792]{1,0:T(8,128)(2,1)S(1)} %get-tuple-element.135.refs_4_), channel_id=1, source_target_pairs={{0,2},{1,3},{2,0},{3,1},{4,6},{5,7},{6,4},{7,5},{8,10},{9,11},{10,... | collective-permute-start | bytes 860168 | tf_op jit(solution)/shard_map/ppermute | solution.py:92
  86.9 6.8 %collective-permute-start.20 = (bf16[80,1792]{1,0:T(8,128)(2,1)S(1)}, bf16[80,1792]{1,0:T(8,128)(2,1)S(1)}, u32[]{:S(2)}, u32[]{:S(2)}) collective-permute-start(bf16[80,1792]{1,0:T(8,128)(2,1)S(1)} %get-tuple-element.136.refs_5_), channel_id=1, source_target_pairs={{2,4},{3,5},{4,2},{5,3},{10,12},{11,13},{12,10},{13,11},{18,20},{1... | collective-permute-start | bytes 860168 | tf_op jit(solution)/shard_map/ppermute | solution.py:92
  88.7 5.6 %collective-permute-start.24 = (bf16[80,1792]{1,0:T(8,128)(2,1)S(1)}, bf16[80,1792]{1,0:T(8,128)(2,1)S(1)}, u32[]{:S(2)}, u32[]{:S(2)}) collective-permute-start(bf16[80,1792]{1,0:T(8,128)(2,1)S(1)} %get-tuple-element.145.refs_2_), channel_id=1, source_target_pairs={{0,1},{1,0},{2,3},{3,2},{4,5},{5,4},{6,7},{7,6},{8,9},{9,8},{10,11... | collective-permute-start | bytes 860168 | tf_op jit(solution)/shard_map/ppermute | solution.py:88
  89.5 16.3 %collective-permute-start.31 = (bf16[320,1024]{1,0:T(8,128)(2,1)S(1)}, bf16[320,1024]{1,0:T(8,128)(2,1)S(1)}, u32[]{:S(2)}, u32[]{:S(2)}) collective-permute-start(bf16[320,1024]{1,0:T(8,128)(2,1)S(1)} %get-tuple-element.156.refs_0_), channel_id=1, source_target_pairs={{0,8},{8,0},{16,24},{24,16},{1,9},{9,1},{17,25},{25,17},{2,10},{10... | collective-permute-start | bytes 1966088 | tf_op jit(solution)/shard_map/ppermute | solution.py:449
  90.6 16.0 %collective-permute-start.32 = (bf16[320,1024]{1,0:T(8,128)(2,1)S(1)}, bf16[320,1024]{1,0:T(8,128)(2,1)S(1)}, u32[]{:S(2)}, u32[]{:S(2)}) collective-permute-start(bf16[320,1024]{1,0:T(8,128)(2,1)S(1)} %get-tuple-element.157.refs_2_), channel_id=1, source_target_pairs={{0,16},{8,24},{16,0},{24,8},{1,17},{9,25},{17,1},{25,9},{2,18},{10... | collective-permute-start | bytes 1966088 | tf_op jit(solution)/shard_map/ppermute | solution.py:449
  91.9 8.3 %collective-permute-start.27 = (bf16[80,1792]{1,0:T(8,128)(2,1)S(1)}, bf16[80,1792]{1,0:T(8,128)(2,1)S(1)}, u32[]{:S(2)}, u32[]{:S(2)}) collective-permute-start(bf16[80,1792]{1,0:T(8,128)(2,1)S(1)} %get-tuple-element.152.refs_2_), channel_id=1, source_target_pairs={{0,2},{1,3},{2,0},{3,1},{4,6},{5,7},{6,4},{7,5},{8,10},{9,11},{10,... | collective-permute-start | bytes 860168 | tf_op jit(solution)/shard_map/ppermute | solution.py:92
  93.6 7.8 %collective-permute-start.28 = (bf16[80,1792]{1,0:T(8,128)(2,1)S(1)}, bf16[80,1792]{1,0:T(8,128)(2,1)S(1)}, u32[]{:S(2)}, u32[]{:S(2)}) collective-permute-start(bf16[80,1792]{1,0:T(8,128)(2,1)S(1)} %get-tuple-element.153.refs_3_), channel_id=1, source_target_pairs={{2,4},{3,5},{4,2},{5,3},{10,12},{11,13},{12,10},{13,11},{18,20},{1... | collective-permute-start | bytes 860168 | tf_op jit(solution)/shard_map/ppermute | solution.py:92
  95.0 7.1 %collective-permute-start.29 = (bf16[80,1792]{1,0:T(8,128)(2,1)S(1)}, bf16[80,1792]{1,0:T(8,128)(2,1)S(1)}, u32[]{:S(2)}, u32[]{:S(2)}) collective-permute-start(bf16[80,1792]{1,0:T(8,128)(2,1)S(1)} %get-tuple-element.147.refs_2_), channel_id=1, source_target_pairs={{0,1},{1,0},{2,3},{3,2},{4,5},{5,4},{6,7},{7,6},{8,9},{9,8},{10,11... | collective-permute-start | bytes 860168 | tf_op jit(solution)/shard_map/ppermute | solution.py:88
  100.2 8.4 %collective-permute-start.25 = (bf16[80,1792]{1,0:T(8,128)(2,1)S(1)}, bf16[80,1792]{1,0:T(8,128)(2,1)S(1)}, u32[]{:S(2)}, u32[]{:S(2)}) collective-permute-start(bf16[80,1792]{1,0:T(8,128)(2,1)S(1)} %get-tuple-element.149.refs_2_), channel_id=1, source_target_pairs={{0,2},{1,3},{2,0},{3,1},{4,6},{5,7},{6,4},{7,5},{8,10},{9,11},{10,... | collective-permute-start | bytes 860168 | tf_op jit(solution)/shard_map/ppermute | solution.py:92
  101.5 12.8 %collective-permute-start.26 = (bf16[80,1792]{1,0:T(8,128)(2,1)S(1)}, bf16[80,1792]{1,0:T(8,128)(2,1)S(1)}, u32[]{:S(2)}, u32[]{:S(2)}) collective-permute-start(bf16[80,1792]{1,0:T(8,128)(2,1)S(1)} %get-tuple-element.150.refs_3_), channel_id=1, source_target_pairs={{2,4},{3,5},{4,2},{5,3},{10,12},{11,13},{12,10},{13,11},{18,20},{1... | collective-permute-start | bytes 860168 | tf_op jit(solution)/shard_map/ppermute | solution.py:92
  103.0 12.0 %collective-permute-start.30 = (bf16[80,1792]{1,0:T(8,128)(2,1)S(1)}, bf16[80,1792]{1,0:T(8,128)(2,1)S(1)}, u32[]{:S(2)}, u32[]{:S(2)}) collective-permute-start(bf16[80,1792]{1,0:T(8,128)(2,1)S(1)} %get-tuple-element.155.refs_3_), channel_id=1, source_target_pairs={{0,1},{1,0},{2,3},{3,2},{4,5},{5,4},{6,7},{7,6},{8,9},{9,8},{10,11... | collective-permute-start | bytes 860168 | tf_op jit(solution)/shard_map/ppermute | solution.py:88
  106.9 18.3 %collective-permute-start.39 = (bf16[320,1024]{1,0:T(8,128)(2,1)S(1)}, bf16[320,1024]{1,0:T(8,128)(2,1)S(1)}, u32[]{:S(2)}, u32[]{:S(2)}) collective-permute-start(bf16[320,1024]{1,0:T(8,128)(2,1)S(1)} %get-tuple-element.167.refs_0_), channel_id=1, source_target_pairs={{0,16},{8,24},{16,0},{24,8},{1,17},{9,25},{17,1},{25,9},{2,18},{10... | collective-permute-start | bytes 1966088 | tf_op jit(solution)/shard_map/ppermute | solution.py:449
  108.3 21.3 %collective-permute-start.40 = (bf16[320,1024]{1,0:T(8,128)(2,1)S(1)}, bf16[320,1024]{1,0:T(8,128)(2,1)S(1)}, u32[]{:S(2)}, u32[]{:S(2)}) collective-permute-start(bf16[320,1024]{1,0:T(8,128)(2,1)S(1)} %get-tuple-element.168.refs_2_), channel_id=1, source_target_pairs={{0,8},{8,0},{16,24},{24,16},{1,9},{9,1},{17,25},{25,17},{2,10},{10... | collective-permute-start | bytes 1966088 | tf_op jit(solution)/shard_map/ppermute | solution.py:449
  108.6 12.4 %collective-permute-start.35 = (bf16[80,1792]{1,0:T(8,128)(2,1)S(1)}, bf16[80,1792]{1,0:T(8,128)(2,1)S(1)}, u32[]{:S(2)}, u32[]{:S(2)}) collective-permute-start(bf16[80,1792]{1,0:T(8,128)(2,1)S(1)} %get-tuple-element.163.refs_2_), channel_id=1, source_target_pairs={{0,2},{1,3},{2,0},{3,1},{4,6},{5,7},{6,4},{7,5},{8,10},{9,11},{10,... | collective-permute-start | bytes 860168 | tf_op jit(solution)/shard_map/ppermute | solution.py:92
  114.3 7.8 %collective-permute-start.36 = (bf16[80,1792]{1,0:T(8,128)(2,1)S(1)}, bf16[80,1792]{1,0:T(8,128)(2,1)S(1)}, u32[]{:S(2)}, u32[]{:S(2)}) collective-permute-start(bf16[80,1792]{1,0:T(8,128)(2,1)S(1)} %get-tuple-element.164.refs_3_), channel_id=1, source_target_pairs={{2,4},{3,5},{4,2},{5,3},{10,12},{11,13},{12,10},{13,11},{18,20},{1... | collective-permute-start | bytes 860168 | tf_op jit(solution)/shard_map/ppermute | solution.py:92
  115.6 7.2 %collective-permute-start.37 = (bf16[80,1792]{1,0:T(8,128)(2,1)S(1)}, bf16[80,1792]{1,0:T(8,128)(2,1)S(1)}, u32[]{:S(2)}, u32[]{:S(2)}) collective-permute-start(bf16[80,1792]{1,0:T(8,128)(2,1)S(1)} %get-tuple-element.160.refs_3_), channel_id=1, source_target_pairs={{0,1},{1,0},{2,3},{3,2},{4,5},{5,4},{6,7},{7,6},{8,9},{9,8},{10,11... | collective-permute-start | bytes 860168 | tf_op jit(solution)/shard_map/ppermute | solution.py:88
  121.0 8.9 %collective-permute-start.33 = (bf16[80,1792]{1,0:T(8,128)(2,1)S(1)}, bf16[80,1792]{1,0:T(8,128)(2,1)S(1)}, u32[]{:S(2)}, u32[]{:S(2)}) collective-permute-start(bf16[80,1792]{1,0:T(8,128)(2,1)S(1)} %get-tuple-element.161.refs_2_), channel_id=1, source_target_pairs={{0,2},{1,3},{2,0},{3,1},{4,6},{5,7},{6,4},{7,5},{8,10},{9,11},{10,... | collective-permute-start | bytes 860168 | tf_op jit(solution)/shard_map/ppermute | solution.py:92
  122.1 7.8 %collective-permute-start.34 = (bf16[80,1792]{1,0:T(8,128)(2,1)S(1)}, bf16[80,1792]{1,0:T(8,128)(2,1)S(1)}, u32[]{:S(2)}, u32[]{:S(2)}) collective-permute-start(bf16[80,1792]{1,0:T(8,128)(2,1)S(1)} %get-tuple-element.162.refs_3_), channel_id=1, source_target_pairs={{2,4},{3,5},{4,2},{5,3},{10,12},{11,13},{12,10},{13,11},{18,20},{1... | collective-permute-start | bytes 860168 | tf_op jit(solution)/shard_map/ppermute | solution.py:92
  123.4 6.5 %collective-permute-start.38 = (bf16[80,1792]{1,0:T(8,128)(2,1)S(1)}, bf16[80,1792]{1,0:T(8,128)(2,1)S(1)}, u32[]{:S(2)}, u32[]{:S(2)}) collective-permute-start(bf16[80,1792]{1,0:T(8,128)(2,1)S(1)} %get-tuple-element.166.refs_4_), channel_id=1, source_target_pairs={{0,1},{1,0},{2,3},{3,2},{4,5},{5,4},{6,7},{7,6},{8,9},{9,8},{10,11... | collective-permute-start | bytes 860168 | tf_op jit(solution)/shard_map/ppermute | solution.py:88
  125.2 11.5 %collective-permute-start.42 = (bf16[80,1792]{1,0:T(8,128)(2,1)S(1)}, bf16[80,1792]{1,0:T(8,128)(2,1)S(1)}, u32[]{:S(2)}, u32[]{:S(2)}) collective-permute-start(bf16[80,1792]{1,0:T(8,128)(2,1)S(1)} %get-tuple-element.174.refs_2_), channel_id=1, source_target_pairs={{0,2},{1,3},{2,0},{3,1},{4,6},{5,7},{6,4},{7,5},{8,10},{9,11},{10,... | collective-permute-start | bytes 860168 | tf_op jit(solution)/shard_map/ppermute | solution.py:92
  130.6 6.1 %collective-permute-start.43 = (bf16[80,1792]{1,0:T(8,128)(2,1)S(1)}, bf16[80,1792]{1,0:T(8,128)(2,1)S(1)}, u32[]{:S(2)}, u32[]{:S(2)}) collective-permute-start(bf16[80,1792]{1,0:T(8,128)(2,1)S(1)} %get-tuple-element.171.refs_4_), channel_id=1, source_target_pairs={{0,1},{1,0},{2,3},{3,2},{4,5},{5,4},{6,7},{7,6},{8,9},{9,8},{10,11... | collective-permute-start | bytes 860168 | tf_op jit(solution)/shard_map/ppermute | solution.py:88
  131.0 11.8 %collective-permute-start.41 = (bf16[80,1792]{1,0:T(8,128)(2,1)S(1)}, bf16[80,1792]{1,0:T(8,128)(2,1)S(1)}, u32[]{:S(2)}, u32[]{:S(2)}) collective-permute-start(bf16[80,1792]{1,0:T(8,128)(2,1)S(1)} %get-tuple-element.172.refs_2_), channel_id=1, source_target_pairs={{0,2},{1,3},{2,0},{3,1},{4,6},{5,7},{6,4},{7,5},{8,10},{9,11},{10,... | collective-permute-start | bytes 860168 | tf_op jit(solution)/shard_map/ppermute | solution.py:92
  138.1 4.7 %collective-permute-start.44 = (bf16[80,1792]{1,0:T(8,128)(2,1)S(1)}, bf16[80,1792]{1,0:T(8,128)(2,1)S(1)}, u32[]{:S(2)}, u32[]{:S(2)}) collective-permute-start(bf16[80,1792]{1,0:T(8,128)(2,1)S(1)} %get-tuple-element.177.refs_5_), channel_id=1, source_target_pairs={{0,1},{1,0},{2,3},{3,2},{4,5},{5,4},{6,7},{7,6},{8,9},{9,8},{10,11... | collective-permute-start | bytes 860168 | tf_op jit(solution)/shard_map/ppermute | solution.py:88
  144.3 11.8 %collective-permute-start.45 = (bf16[80,1792]{1,0:T(8,128)(2,1)S(1)}, bf16[80,1792]{1,0:T(8,128)(2,1)S(1)}, u32[]{:S(2)}, u32[]{:S(2)}) collective-permute-start(bf16[80,1792]{1,0:T(8,128)(2,1)S(1)} %get-tuple-element.179.refs_5_), channel_id=1, source_target_pairs={{0,1},{1,0},{2,3},{3,2},{4,5},{5,4},{6,7},{7,6},{8,9},{9,8},{10,11... | collective-permute-start | bytes 860168 | tf_op jit(solution)/shard_map/ppermute | solution.py:88
Sparse Core Ops, SparseCore 0:
  10.3 41.7 all-gather.2
where the time goes:
time: 174 us; the launch traced here: 173 us
  Pallas kernels  72.5 us (42%)
  starting transfers between devices  57 us (33%)
  waiting for transfers between devices  28.9 us (17%)
  between operations  15 us (9%)
    pallas_call x24, Pallas kernels, call(): pl.pallas_call(body, in_specs=in_specs + [anywhere] * len(tokens), out_sp...  72.5 us
    ppermute x20, starting transfers between devices, move_chip(): lax.ppermute(x, 'mp', [(HALVES * a + c, HALVES * b + c) for a, b in pairs...  34 us
    ppermute x20, waiting for transfers between devices, move_chip(): lax.ppermute(x, 'mp', [(HALVES * a + c, HALVES * b + c) for a, b in pairs...  25.8 us
    ppermute x16, starting transfers between devices, swap_core(): return lax.ppermute(x, 'mp', [(i, i ^ 1) for i in range(size)])  13 us
    ppermute x6, starting transfers between devices, swap_quarter(): return lax.ppermute(x, 'dp', [(i, i ^ step) for i in range(size)])  5.95 us
    ppermute x4, starting transfers between devices, send(): lax.ppermute(x, 'dp', [(i, i ^ step) for i in range(self.size)])  4.11 us
  transfers between devices with their start and end apart: 47, of which 9 were waited for; matrix products, arithmetic and copies ran while one was open for 0% of the time, Pallas kernels for 33%

commit v1 on v0

--- a/solution.py
+++ b/solution.py
@@ -15,12 +15,6 @@
 
 def tile_of(width, limit):
     return max(t for t in range(LANES, limit + 1, LANES) if width % t == 0)
-
-
-def contract_rows(left, right):
-    return lax.dot_general(
-        left, right, (((0,), (0,)), ((), ())), preferred_element_type=jnp.float32
-    )
 
 
 def streams_of(width):
@@ -342,37 +336,53 @@
     queries = rot_refs[0].shape[0] - tokens
     quarter, core = place_ref[0], place_ref[1]
 
-    def put(tok, qry, piece, values):
-        tok[pl.ds(pl.multiple_of(piece * tokens, 16), tokens), :] = values[:tokens]
-        qry[pl.ds(pl.multiple_of(piece * queries, 16), queries), :] = values[tokens:]
+    def put(piece, values):
+        rot_tok[pl.ds(pl.multiple_of(piece * tokens, 16), tokens), :] = values[:tokens]
+        rot_qry[pl.ds(pl.multiple_of(piece * queries, 16), queries), :] = values[tokens:]
 
     @pl.when(pl.program_id(0) == 0)
     def _():
         per_ref = PIECES // HALVES
         size = tokens + queries
+        act_qry[...] = jnp.zeros_like(act_qry)
         for piece in range(PIECES):
-            at = piece % per_ref * size
-            put(act_tok, act_qry, piece, act_refs[piece // per_ref][at:at + size, :])
+            ref, at = act_refs[piece // per_ref], piece % per_ref * size
+            row = piece * tokens
+            act_tok[row:row + tokens, :] = ref[at:at + tokens, :]
+            row = piece * queries
+            act_qry[piece // HALVES, row:row + queries, :] = ref[at + tokens:at + size, :]
 
     for held, refs_held in ((core, rot_refs[:QUARTERS]), (1 - core, rot_refs[QUARTERS:])):
         for (bits, half), ref in zip(rotated_places(held), refs_held):
-            put(rot_tok, rot_qry, (quarter ^ bits) * HALVES + half, ref[...])
+            put((quarter ^ bits) * HALVES + half, ref[...])
 
     length = tokens * PIECES // 2
-    total = None
-    for seq in range(2):
-        rows = slice(seq * length, (seq + 1) * length)
-        rotated = contract_rows(rot_tok[rows, :], act_tok[rows, :])
-        square = rotated * rotated
-        total = square if total is None else total + square
-    eig = total * (1.0 / (2 * length))
-    eig_ref[...] = eig
-    inverse = 1.0 / (eig + damping_ref[0])
-    rank = queries * HALVES
-    for query in range(QUARTERS):
-        rows = slice(query * rank, (query + 1) * rank)
-        product = contract_rows(rot_qry[rows, :], act_qry[rows, :])
-        pre_ref[query] = (product * inverse).astype(pre_ref.dtype)
+    outs, ins = eig_ref.shape
+    token_rows, query_rows = rot_tok[...].T, rot_qry[...].T
+    down, across = tile_of(outs, 128), tile_of(ins, 256)
+    for at in range(0, outs, down):
+        for by in range(0, ins, across):
+            rows, columns = slice(at, at + down), slice(by, by + across)
+            total = None
+            for seq in range(2):
+                span = slice(seq * length, (seq + 1) * length)
+                rotated = jnp.dot(
+                    token_rows[rows, span],
+                    act_tok[span, columns],
+                    preferred_element_type=jnp.float32,
+                )
+                square = rotated * rotated
+                total = square if total is None else total + square
+            eig = total * (1.0 / (2 * length))
+            eig_ref[rows, columns] = eig
+            inverse = 1.0 / (eig + damping_ref[0])
+            for query in range(QUARTERS):
+                product = jnp.dot(
+                    query_rows[rows],
+                    act_qry[query, :, columns],
+                    preferred_element_type=jnp.float32,
+                )
+                pre_ref[query, rows, columns] = (product * inverse).astype(pre_ref.dtype)
 
 
 def correct(order, tokens, place, damping, rot, act, block, outs, made):
@@ -406,7 +416,7 @@
             pltpu.VMEM((PIECES * tokens, tile), dtype),
             pltpu.VMEM((PIECES * queries, tile), dtype),
             pltpu.VMEM((PIECES * tokens, ins), dtype),
-            pltpu.VMEM((PIECES * queries, ins), dtype),
+            pltpu.VMEM((QUARTERS, PIECES * queries, ins), dtype),
         ],
         vmem=32 * MIB,
         name="correct",
@@ -525,15 +535,15 @@
     rotate(across, [*across])
     advance(0)
     advance(1)
+    advance(0)
+    advance(1)
     activate()
     advance(0)
     advance(1)
-    advance(0)
     acts.add(order)
-    advance(1)
-    advance(0)
+    advance(0)
+    advance(1)
     acts.add(order)
-    advance(1)
     advance(0)
     advance(1)
     while acts.hop < len(acts.hops):

time: 174 us -> 175 us (level)
  starting transfers between devices: 57 us -> 61.8 us
  waiting for transfers between devices: 28.9 us -> 24.6 us
    ppermute x20, waiting for transfers between devices: 25.8 us -> 21.6 us  [move_chip(): lax.ppermute(x, 'mp', [(HALVES * a + c, HALVES * b + c) for a, b in pairs...]
    ppermute x16, starting transfers between devices: 13 us -> 16.4 us  [swap_core(): return lax.ppermute(x, 'mp', [(i, i ^ 1) for i in range(size)])]
    ppermute x20, starting transfers between devices: 34 us -> 37 us  [move_chip(): lax.ppermute(x, 'mp', [(HALVES * a + c, HALVES * b + c) for a, b in pairs...]
    ppermute x6, waiting for transfers between devices: 0.02 us -> 2.05 us  [swap_quarter(): return lax.ppermute(x, 'dp', [(i, i ^ step) for i in range(size)])]
    ppermute x4, waiting for transfers between devices: 1.84 us -> 0.01 us  [send(): lax.ppermute(x, 'dp', [(i, i ^ step) for i in range(self.size)])]
where the time goes in v1:
time: 175 us
  Pallas kernels  73.2 us (42%)
  starting transfers between devices  61.8 us (35%)
  waiting for transfers between devices  24.6 us (14%)
  between operations  15 us (9%)
    pallas_call x24, Pallas kernels, call(): pl.pallas_call(body, in_specs=in_specs + [anywhere] * len(tokens), out_sp...  73.2 us
    ppermute x20, starting transfers between devices, move_chip(): lax.ppermute(x, 'mp', [(HALVES * a + c, HALVES * b + c) for a, b in pairs...  37 us
    ppermute x20, waiting for transfers between devices, move_chip(): lax.ppermute(x, 'mp', [(HALVES * a + c, HALVES * b + c) for a, b in pairs...  21.6 us
    ppermute x16, starting transfers between devices, swap_core(): return lax.ppermute(x, 'mp', [(i, i ^ 1) for i in range(size)])  16.4 us
    ppermute x6, starting transfers between devices, swap_quarter(): return lax.ppermute(x, 'dp', [(i, i ^ step) for i in range(size)])  4.77 us
    ppermute x4, starting transfers between devices, send(): lax.ppermute(x, 'dp', [(i, i ^ step) for i in range(self.size)])  3.69 us
  transfers between devices with their start and end apart: 47, of which 9 were waited for; matrix products, arithmetic and copies ran while one was open for 0% of the time, Pallas kernels for 33%

profile of v1, /device:TPU:1, one launch (start us, length us, event | category | flops | bytes accessed | tf_op | source)
XLA Modules:
  0.0 174.7 jit_solution(12871707399841396055)
XLA Ops:
  7.2 2.9 %join_rows.1 = (bf16[80,3584]{1,0:T(8,128)(2,1)S(1)}, bf16[80,3584]{1,0:T(8,128)(2,1)S(1)}, bf16[80,2048]{1,0:T(8,128)(2,1)}, f32[8,128]{1,0:T(8,128)S(1)}) custom-call(bf16[128,3584]{1,0:T(8,128)(2,1)} %refs_0_.1, bf16[32,3584]{1,0:T(8,128)(2,1)} %refs_1_.4, bf16[64,2048]{1,0:T(8,128)(2,1)} %refs_2_.1, bf16[16,2048]{1,0:T(8,128)(2,1)} %refs_3_.2), custom_call_target="tpu_custom_call" | custom-call | tf_op jit(solution)/shard_map/join_rows/pallas_call | solution.py:52
  10.2 2.1 %collective-permute-start = (bf16[80,3584]{1,0:T(8,128)(2,1)S(1)}, bf16[80,3584]{1,0:T(8,128)(2,1)S(1)}, u32[]{:S(2)}, u32[]{:S(2)}) collective-permute-start(bf16[80,3584]{1,0:T(8,128)(2,1)S(1)} %get-tuple-element.95.refs_1_), channel_id=1, source_target_pairs={{0,16},{8,24},{16,0},{24,8},{1,17},{9,25},{17,1},{25,9},{2,18},{10... | collective-permute-start | bytes 1720328 | tf_op jit(solution)/shard_map/ppermute | solution.py:77
  12.3 1.2 collective-permute-start.2
  13.6 10.3 %load_and_multiply.1 = (bf16[80,1792]{1,0:T(8,128)(2,1)S(1)}, bf16[80,1792]{1,0:T(8,128)(2,1)S(1)}, bf16[80,1792]{1,0:T(8,128)(2,1)S(1)}, bf16[80,1792]{1,0:T(8,...) custom-call(s32[3]{0:T(128)S(1)} %pad_add_fusion.refs_0_, ...), custom_call_target="tpu_custom_call" | custom-call | tf_op jit(solution)/shard_map/load_and_multiply/pallas_call | solution.py:52
  23.9 1.3 collective-permute-start.5
  25.5 0.9 collective-permute-done.5.refs_2_
  26.6 1.4 line_step.14
  28.0 1.4 collective-permute-start.11
  29.4 1.4 line_step.15
  30.8 5.0 %multiply.3 = (bf16[80,1792]{1,0:T(8,128)(2,1)S(1)}, bf16[80,1792]{1,0:T(8,128)(2,1)S(1)}, bf16[80,1792]{1,0:T(8,128)(2,1)S(1)}, bf16[80,1792]{1,0:T(8,128)(2,1)S(1)}, f32[8,128]{1,0:T(8,128)S(1)}) custom-call(s32[3]{0:T(128)S(1)} %pad_add_fusion.refs_0_, bf16[80,3584]{1,0:T(8,128)(2,1)S(1)} %collective-permute-done.refs_1_, ...), custom_call_target="tpu_custom_call" | custom-call | tf_op jit(solution)/shard_map/multiply/pallas_call | solution.py:52
  35.8 1.0 collective-permute-start.10
  36.8 0.7 collective-permute-start.1
  37.5 2.0 %collective-permute-done.8.refs_1_.refs_4_ = bf16[80,3584]{1,0:T(8,128)(2,1)S(1)} collective-permute-done((bf16[80,3584]{1,0:T(8,128)(2,1)S(1)}, bf16[80,3584]{1,0:T(8,128)(2,1)S(1)}, u32[]{:S(2)}, u32[]{:S(2)}) %collective-permute-start.8) | collective-permute-done | bytes 573472 | tf_op jit(solution)/shard_map/ppermute | solution.py:77
  39.7 10.3 %collective-permute-done.11.refs_6_ = bf16[80,1792]{1,0:T(8,128)(2,1)S(1)} collective-permute-done((bf16[80,1792]{1,0:T(8,128)(2,1)S(1)}, bf16[80,1792]{1,0:T(8,128)(2,1)S(1)}, u32[]{:S(2)}, u32[]{:S(2)}) %collective-permute-start.11) | collective-permute-done | bytes 286752 | tf_op jit(solution)/shard_map/ppermute | solution.py:86
  50.6 1.6 line_step.16
  52.1 5.0 %multiply.4 = (bf16[80,1792]{1,0:T(8,128)(2,1)S(1)}, bf16[80,1792]{1,0:T(8,128)(2,1)S(1)}, bf16[80,1792]{1,0:T(8,128)(2,1)S(1)}, bf16[80,1792]{1,0:T(8,128)(2,1)S(1)}, f32[8,128]{1,0:T(8,128)S(1)}) custom-call(s32[3]{0:T(128)S(1)} %pad_add_fusion.refs_0_, bf16[80,3584]{1,0:T(8,128)(2,1)S(1)} %collective-permute-done.8.refs_1_.refs_4_, ...), custom_call_target="tpu_custom_call" | custom-call | tf_op jit(solution)/shard_map/multiply/pallas_call | solution.py:52
  57.2 0.7 collective-permute-done.7.refs_6_
  57.9 1.2 collective-permute-start.17
  59.1 0.7 collective-permute-start.18
  59.8 0.8 collective-permute-start.13
  60.5 1.4 line_step.17
  61.9 4.1 %collective-permute-start.14 = (bf16[80,1792]{1,0:T(8,128)(2,1)S(1)}, bf16[80,1792]{1,0:T(8,128)(2,1)S(1)}, u32[]{:S(2)}, u32[]{:S(2)}) collective-permute-start(bf16[80,1792]{1,0:T(8,128)(2,1)S(1)} %get-tuple-element.125.refs_4_), channel_id=1, source_target_pairs={{0,2},{1,3},{2,0},{3,1},{4,6},{5,7},{6,4},{7,5},{8,10},{9,11},{10,... | collective-permute-start | bytes 860168 | tf_op jit(solution)/shard_map/ppermute | solution.py:86
  66.0 5.0 %multiply.5 = (bf16[80,1792]{1,0:T(8,128)(2,1)S(1)}, bf16[80,1792]{1,0:T(8,128)(2,1)S(1)}, bf16[80,1792]{1,0:T(8,128)(2,1)S(1)}, bf16[80,1792]{1,0:T(8,128)(2,1)S(1)}, f32[8,128]{1,0:T(8,128)S(1)}) custom-call(s32[3]{0:T(128)S(1)} %pad_add_fusion.refs_0_, bf16[80,3584]{1,0:T(8,128)(2,1)S(1)} %collective-permute-done.1.refs_1_.refs_4_, ...), custom_call_target="tpu_custom_call" | custom-call | tf_op jit(solution)/shard_map/multiply/pallas_call | solution.py:52
  71.0 0.7 collective-permute-start.15
  71.7 1.4 line_step.18
  73.1 1.6 collective-permute-start.22
  74.7 0.7 collective-permute-start.23
  75.3 0.6 collective-permute-start.21
  76.1 1.4 line_step.19
  77.5 5.3 %collective-permute-start.19 = (bf16[80,1792]{1,0:T(8,128)(2,1)S(1)}, bf16[80,1792]{1,0:T(8,128)(2,1)S(1)}, u32[]{:S(2)}, u32[]{:S(2)}) collective-permute-start(bf16[80,1792]{1,0:T(8,128)(2,1)S(1)} %get-tuple-element.135.refs_4_), channel_id=1, source_target_pairs={{0,2},{1,3},{2,0},{3,1},{4,6},{5,7},{6,4},{7,5},{8,10},{9,11},{10,... | collective-permute-start | bytes 860168 | tf_op jit(solution)/shard_map/ppermute | solution.py:86
  82.8 0.7 collective-permute-start.20
  83.5 0.7 line_step.20
  84.2 1.5 collective-permute-start.24
  85.7 3.8 %collective-permute-start.27 = (bf16[80,1792]{1,0:T(8,128)(2,1)S(1)}, bf16[80,1792]{1,0:T(8,128)(2,1)S(1)}, u32[]{:S(2)}, u32[]{:S(2)}) collective-permute-start(bf16[80,1792]{1,0:T(8,128)(2,1)S(1)} %get-tuple-element.150.refs_2_), channel_id=1, source_target_pairs={{0,2},{1,3},{2,0},{3,1},{4,6},{5,7},{6,4},{7,5},{8,10},{9,11},{10,... | collective-permute-start | bytes 860168 | tf_op jit(solution)/shard_map/ppermute | solution.py:86
  89.5 0.7 collective-permute-start.28
  90.2 0.7 line_step.21
  91.4 6.0 %multiply_activations.1 = (bf16[320,1024]{1,0:T(8,128)(2,1)S(1)}, bf16[320,1024]{1,0:T(8,128)(2,1)S(1)}, f32[8,128]{1,0:T(8,128)S(1)}) custom-call(bf16[640,2048]{1,0:T(8,128)(2,1)} %all-gather.3.cloned.1.call-done.refs_0_, bf16[2048,1024]{1,0:T(8,128)(2,1)} %refs_1_.5, f32[8,128]{1,0:T(8,128)S(1)} %get-tuple-element.153.refs_2_), custom_call_target="tpu_custom_call" | custom-call | tf_op jit(solution)/shard_map/multiply_activations/pallas_call | solution.py:52
  97.4 1.2 collective-permute-start.36
  98.6 1.3 collective-permute-start.37
  99.9 3.9 %collective-permute-start.25 = (bf16[80,1792]{1,0:T(8,128)(2,1)S(1)}, bf16[80,1792]{1,0:T(8,128)(2,1)S(1)}, u32[]{:S(2)}, u32[]{:S(2)}) collective-permute-start(bf16[80,1792]{1,0:T(8,128)(2,1)S(1)} %get-tuple-element.147.refs_2_), channel_id=1, source_target_pairs={{0,2},{1,3},{2,0},{3,1},{4,6},{5,7},{6,4},{7,5},{8,10},{9,11},{10,... | collective-permute-start | bytes 860168 | tf_op jit(solution)/shard_map/ppermute | solution.py:86
  103.8 0.7 collective-permute-start.26
  105.1 1.0 collective-permute-start.30
  106.1 4.3 %collective-permute-done.25.refs_4_ = bf16[80,1792]{1,0:T(8,128)(2,1)S(1)} collective-permute-done((bf16[80,1792]{1,0:T(8,128)(2,1)S(1)}, bf16[80,1792]{1,0:T(8,128)(2,1)S(1)}, u32[]{:S(2)}, u32[]{:S(2)}) %collective-permute-start.25) | collective-permute-done | bytes 286752 | tf_op jit(solution)/shard_map/ppermute | solution.py:86
  110.4 1.1 collective-permute-start.33
  111.6 0.7 collective-permute-start.34
  112.2 0.8 line_step.23
  113.1 1.8 %collective-permute-start.35 = (bf16[80,1792]{1,0:T(8,128)(2,1)S(1)}, bf16[80,1792]{1,0:T(8,128)(2,1)S(1)}, u32[]{:S(2)}, u32[]{:S(2)}) collective-permute-start(bf16[80,1792]{1,0:T(8,128)(2,1)S(1)} %get-tuple-element.157.refs_3_), channel_id=1, source_target_pairs={{0,1},{1,0},{2,3},{3,2},{4,5},{5,4},{6,7},{7,6},{8,9},{9,8},{10,11... | collective-permute-start | bytes 860168 | tf_op jit(solution)/shard_map/ppermute | solution.py:82
  115.3 0.9 collective-permute-start.42
  116.5 1.1 collective-permute-done.33.refs_4_
  117.6 2.9 %collective-permute-start.31 = (bf16[80,1792]{1,0:T(8,128)(2,1)S(1)}, bf16[80,1792]{1,0:T(8,128)(2,1)S(1)}, u32[]{:S(2)}, u32[]{:S(2)}) collective-permute-start(bf16[80,1792]{1,0:T(8,128)(2,1)S(1)} %get-tuple-element.158.refs_2_), channel_id=1, source_target_pairs={{0,2},{1,3},{2,0},{3,1},{4,6},{5,7},{6,4},{7,5},{8,10},{9,11},{10,... | collective-permute-start | bytes 860168 | tf_op jit(solution)/shard_map/ppermute | solution.py:86
  120.5 0.7 collective-permute-start.32
  121.2 0.6 line_step.24
  121.8 2.0 %collective-permute-start.38 = (bf16[80,1792]{1,0:T(8,128)(2,1)S(1)}, bf16[80,1792]{1,0:T(8,128)(2,1)S(1)}, u32[]{:S(2)}, u32[]{:S(2)}) collective-permute-start(bf16[80,1792]{1,0:T(8,128)(2,1)S(1)} %get-tuple-element.166.refs_4_), channel_id=1, source_target_pairs={{0,1},{1,0},{2,3},{3,2},{4,5},{5,4},{6,7},{7,6},{8,9},{9,8},{10,11... | collective-permute-start | bytes 860168 | tf_op jit(solution)/shard_map/ppermute | solution.py:82
  123.8 2.1 %collective-permute-done.31.refs_4_ = bf16[80,1792]{1,0:T(8,128)(2,1)S(1)} collective-permute-done((bf16[80,1792]{1,0:T(8,128)(2,1)S(1)}, bf16[80,1792]{1,0:T(8,128)(2,1)S(1)}, u32[]{:S(2)}, u32[]{:S(2)}) %collective-permute-start.31) | collective-permute-done | bytes 286752 | tf_op jit(solution)/shard_map/ppermute | solution.py:86
  125.9 3.0 %collective-permute-start.40 = (bf16[80,1792]{1,0:T(8,128)(2,1)S(1)}, bf16[80,1792]{1,0:T(8,128)(2,1)S(1)}, u32[]{:S(2)}, u32[]{:S(2)}) collective-permute-start(bf16[80,1792]{1,0:T(8,128)(2,1)S(1)} %get-tuple-element.171.refs_2_), channel_id=1, source_target_pairs={{0,2},{1,3},{2,0},{3,1},{4,6},{5,7},{6,4},{7,5},{8,10},{9,11},{10,... | collective-permute-start | bytes 860168 | tf_op jit(solution)/shard_map/ppermute | solution.py:86
  129.5 1.2 collective-permute-start.41
  130.7 3.4 %collective-permute-start.39 = (bf16[80,1792]{1,0:T(8,128)(2,1)S(1)}, bf16[80,1792]{1,0:T(8,128)(2,1)S(1)}, u32[]{:S(2)}, u32[]{:S(2)}) collective-permute-start(bf16[80,1792]{1,0:T(8,128)(2,1)S(1)} %get-tuple-element.169.refs_2_), channel_id=1, source_target_pairs={{0,2},{1,3},{2,0},{3,1},{4,6},{5,7},{6,4},{7,5},{8,10},{9,11},{10,... | collective-permute-start | bytes 860168 | tf_op jit(solution)/shard_map/ppermute | solution.py:86
  134.9 1.4 line_step.26
  136.4 2.6 %collective-permute-start.44 = (bf16[80,1792]{1,0:T(8,128)(2,1)S(1)}, bf16[80,1792]{1,0:T(8,128)(2,1)S(1)}, u32[]{:S(2)}, u32[]{:S(2)}) collective-permute-start(bf16[80,1792]{1,0:T(8,128)(2,1)S(1)} %get-tuple-element.177.refs_5_), channel_id=1, source_target_pairs={{0,1},{1,0},{2,3},{3,2},{4,5},{5,4},{6,7},{7,6},{8,9},{9,8},{10,11... | collective-permute-start | bytes 860168 | tf_op jit(solution)/shard_map/ppermute | solution.py:82
  139.0 2.6 %collective-permute-done.39.refs_4_ = bf16[80,1792]{1,0:T(8,128)(2,1)S(1)} collective-permute-done((bf16[80,1792]{1,0:T(8,128)(2,1)S(1)}, bf16[80,1792]{1,0:T(8,128)(2,1)S(1)}, u32[]{:S(2)}, u32[]{:S(2)}) %collective-permute-start.39) | collective-permute-done | bytes 286752 | tf_op jit(solution)/shard_map/ppermute | solution.py:86
  141.6 1.4 line_step.27
  143.0 1.3 collective-permute-start.45
  144.9 11.5 %correct.2 = (f32[3584,1024]{1,0:T(8,128)}, bf16[4,3584,1024]{2,1,0:T(8,128)(2,1)}, f32[8,128]{1,0:T(8,128)S(1)}) custom-call(s32[3]{0:T(128)S(1)} %pad_add_fusion.refs_0_, f32[1]{0:T(128)S(6)} %copy.13.refs_1_, bf16[80,1792]{1,0:T(8,128)(2,1)S(1)} %get-tuple-element.143.refs_2_, bf16[80,1792]{1,0:T(8,128)(2,1)S(1)} %get-tuple-element.155.refs_3_, ...), custom_call_target="tpu_custom_call" | custom-call | tf_op jit(solution)/shard_map/correct/pallas_call | solution.py:52
  156.4 11.5 %correct.3 = (f32[3584,1024]{1,0:T(8,128)}, bf16[4,3584,1024]{2,1,0:T(8,128)(2,1)}, f32[8,128]{1,0:T(8,128)}) custom-call(s32[3]{0:T(128)S(1)} %pad_add_fusion.refs_0_, f32[1]{0:T(128)S(6)} %copy.13.refs_1_, bf16[80,1792]{1,0:T(8,128)(2,1)S(1)} %get-tuple-element.145.refs_2_, ...), custom_call_target="tpu_custom_call", output_to_operand_aliasing={{0}: (12, {}), {1}: (13, {})} | custom-call | tf_op jit(solution)/shard_map/correct/pallas_call | solution.py:52
  (56 shorter events, 4.8 us)
Async XLA Ops:
  7.2 84.2 %all-gather.3.cloned.1.call-start = ((), (), s32[]{:S(2)}) async-start(), calls=%async_computation | async-start | bytes 2949120 | tf_op jit(solution)/shard_map/all_gather | solution.py:471
  10.2 20.6 %collective-permute-start = (bf16[80,3584]{1,0:T(8,128)(2,1)S(1)}, bf16[80,3584]{1,0:T(8,128)(2,1)S(1)}, u32[]{:S(2)}, u32[]{:S(2)}) collective-permute-start(bf16[80,3584]{1,0:T(8,128)(2,1)S(1)} %get-tuple-element.95.refs_1_), channel_id=1, source_target_pairs={{0,16},{8,24},{16,0},{24,8},{1,17},{9,25},{17,1},{25,9},{2,18},{10... | collective-permute-start | bytes 1720328 | tf_op jit(solution)/shard_map/ppermute | solution.py:77
  12.3 18.5 %collective-permute-start.2 = (bf16[80,3584]{1,0:T(8,128)(2,1)S(1)}, bf16[80,3584]{1,0:T(8,128)(2,1)S(1)}, u32[]{:S(2)}, u32[]{:S(2)}) collective-permute-start(bf16[80,3584]{1,0:T(8,128)(2,1)S(1)} %get-tuple-element.96.refs_2_), channel_id=1, source_target_pairs={{0,8},{8,0},{16,24},{24,16},{1,9},{9,1},{17,25},{25,17},{2,10},{10... | collective-permute-start | bytes 1720328 | tf_op jit(solution)/shard_map/ppermute | solution.py:77
  23.9 2.5 %collective-permute-start.5 = (bf16[80,1792]{1,0:T(8,128)(2,1)S(1)}, bf16[80,1792]{1,0:T(8,128)(2,1)S(1)}, u32[]{:S(2)}, u32[]{:S(2)}) collective-permute-start(bf16[80,1792]{1,0:T(8,128)(2,1)S(1)} %get-tuple-element.102), channel_id=1, source_target_pairs={{0,1},{1,0},{2,3},{3,2},{4,5},{5,4},{6,7},{7,6},{8,9},{9,8},{10,11... | collective-permute-start | bytes 860168 | tf_op jit(solution)/shard_map/ppermute | solution.py:82
  25.2 2.8 %collective-permute-start.4 = (bf16[80,1792]{1,0:T(8,128)(2,1)S(1)}, bf16[80,1792]{1,0:T(8,128)(2,1)S(1)}, u32[]{:S(2)}, u32[]{:S(2)}) collective-permute-start(bf16[80,1792]{1,0:T(8,128)(2,1)S(1)} %get-tuple-element.100), channel_id=1, source_target_pairs={{0,1},{1,0},{2,3},{3,2},{4,5},{5,4},{6,7},{7,6},{8,9},{9,8},{10,11... | collective-permute-start | bytes 860168 | tf_op jit(solution)/shard_map/ppermute | solution.py:82
  25.3 14.2 %collective-permute-start.8 = (bf16[80,3584]{1,0:T(8,128)(2,1)S(1)}, bf16[80,3584]{1,0:T(8,128)(2,1)S(1)}, u32[]{:S(2)}, u32[]{:S(2)}) collective-permute-start(bf16[80,3584]{1,0:T(8,128)(2,1)S(1)} %get-tuple-element.95.refs_1_), channel_id=1, source_target_pairs={{0,8},{8,0},{16,24},{24,16},{1,9},{9,1},{17,25},{25,17},{2,10},{10... | collective-permute-start | bytes 1720328 | tf_op jit(solution)/shard_map/ppermute | solution.py:77
  26.4 25.7 %collective-permute-start.9 = (bf16[80,3584]{1,0:T(8,128)(2,1)S(1)}, bf16[80,3584]{1,0:T(8,128)(2,1)S(1)}, u32[]{:S(2)}, u32[]{:S(2)}) collective-permute-start(bf16[80,3584]{1,0:T(8,128)(2,1)S(1)} %get-tuple-element.96.refs_2_), channel_id=1, source_target_pairs={{0,16},{8,24},{16,0},{24,8},{1,17},{9,25},{17,1},{25,9},{2,18},{10... | collective-permute-start | bytes 1720328 | tf_op jit(solution)/shard_map/ppermute | solution.py:77
  28.0 22.0 %collective-permute-start.11 = (bf16[80,1792]{1,0:T(8,128)(2,1)S(1)}, bf16[80,1792]{1,0:T(8,128)(2,1)S(1)}, u32[]{:S(2)}, u32[]{:S(2)}) collective-permute-start(bf16[80,1792]{1,0:T(8,128)(2,1)S(1)} %get-tuple-element.114.refs_4_), channel_id=1, source_target_pairs={{0,2},{1,3},{2,0},{3,1},{4,6},{5,7},{6,4},{7,5},{8,10},{9,11},{10,... | collective-permute-start | bytes 860168 | tf_op jit(solution)/shard_map/ppermute | solution.py:86
  35.8 14.3 %collective-permute-start.10 = (bf16[80,1792]{1,0:T(8,128)(2,1)S(1)}, bf16[80,1792]{1,0:T(8,128)(2,1)S(1)}, u32[]{:S(2)}, u32[]{:S(2)}) collective-permute-start(bf16[80,1792]{1,0:T(8,128)(2,1)S(1)} %get-tuple-element.112), channel_id=1, source_target_pairs={{0,1},{1,0},{2,3},{3,2},{4,5},{5,4},{6,7},{7,6},{8,9},{9,8},{10,11... | collective-permute-start | bytes 860168 | tf_op jit(solution)/shard_map/ppermute | solution.py:82
  36.8 23.0 %collective-permute-start.1 = (bf16[80,3584]{1,0:T(8,128)(2,1)S(1)}, bf16[80,3584]{1,0:T(8,128)(2,1)S(1)}, u32[]{:S(2)}, u32[]{:S(2)}) collective-permute-start(bf16[80,3584]{1,0:T(8,128)(2,1)S(1)} %collective-permute-done.refs_1_), channel_id=1, source_target_pairs={{0,8},{8,0},{16,24},{24,16},{1,9},{9,1},{17,25},{25,17},{2,10},{10... | collective-permute-start | bytes 1720328 | tf_op jit(solution)/shard_map/ppermute | solution.py:77
  39.5 22.4 %collective-permute-start.3 = (bf16[80,3584]{1,0:T(8,128)(2,1)S(1)}, bf16[80,3584]{1,0:T(8,128)(2,1)S(1)}, u32[]{:S(2)}, u32[]{:S(2)}) collective-permute-start(bf16[80,3584]{1,0:T(8,128)(2,1)S(1)} %collective-permute-done.2.refs_2_), channel_id=1, source_target_pairs={{0,16},{8,24},{16,0},{24,8},{1,17},{9,25},{17,1},{25,9},{2,18},{10... | collective-permute-start | bytes 1720328 | tf_op jit(solution)/shard_map/ppermute | solution.py:77
  50.0 7.9 %collective-permute-start.7 = (bf16[80,1792]{1,0:T(8,128)(2,1)S(1)}, bf16[80,1792]{1,0:T(8,128)(2,1)S(1)}, u32[]{:S(2)}, u32[]{:S(2)}) collective-permute-start(bf16[80,1792]{1,0:T(8,128)(2,1)S(1)} %get-tuple-element.109.refs_4_), channel_id=1, source_target_pairs={{0,2},{1,3},{2,0},{3,1},{4,6},{5,7},{6,4},{7,5},{8,10},{9,11},{10,... | collective-permute-start | bytes 860168 | tf_op jit(solution)/shard_map/ppermute | solution.py:86
  50.0 9.0 %collective-permute-start.6 = (bf16[80,1792]{1,0:T(8,128)(2,1)S(1)}, bf16[80,1792]{1,0:T(8,128)(2,1)S(1)}, u32[]{:S(2)}, u32[]{:S(2)}) collective-permute-start(bf16[80,1792]{1,0:T(8,128)(2,1)S(1)} %get-tuple-element.107), channel_id=1, source_target_pairs={{0,1},{1,0},{2,3},{3,2},{4,5},{5,4},{6,7},{7,6},{8,9},{9,8},{10,11... | collective-permute-start | bytes 860168 | tf_op jit(solution)/shard_map/ppermute | solution.py:82
  57.1 13.9 %collective-permute-start.16 = (bf16[80,1792]{1,0:T(8,128)(2,1)S(1)}, bf16[80,1792]{1,0:T(8,128)(2,1)S(1)}, u32[]{:S(2)}, u32[]{:S(2)}) collective-permute-start(bf16[80,1792]{1,0:T(8,128)(2,1)S(1)} %get-tuple-element.128), channel_id=1, source_target_pairs={{0,1},{1,0},{2,3},{3,2},{4,5},{5,4},{6,7},{7,6},{8,9},{9,8},{10,11... | collective-permute-start | bytes 860168 | tf_op jit(solution)/shard_map/ppermute | solution.py:82
  57.9 13.8 %collective-permute-start.17 = (bf16[80,1792]{1,0:T(8,128)(2,1)S(1)}, bf16[80,1792]{1,0:T(8,128)(2,1)S(1)}, u32[]{:S(2)}, u32[]{:S(2)}) collective-permute-start(bf16[80,1792]{1,0:T(8,128)(2,1)S(1)} %get-tuple-element.130.refs_4_), channel_id=1, source_target_pairs={{0,2},{1,3},{2,0},{3,1},{4,6},{5,7},{6,4},{7,5},{8,10},{9,11},{10,... | collective-permute-start | bytes 860168 | tf_op jit(solution)/shard_map/ppermute | solution.py:86
  59.1 12.6 %collective-permute-start.18 = (bf16[80,1792]{1,0:T(8,128)(2,1)S(1)}, bf16[80,1792]{1,0:T(8,128)(2,1)S(1)}, u32[]{:S(2)}, u32[]{:S(2)}) collective-permute-start(bf16[80,1792]{1,0:T(8,128)(2,1)S(1)} %get-tuple-element.131.refs_5_), channel_id=1, source_target_pairs={{2,4},{3,5},{4,2},{5,3},{10,12},{11,13},{12,10},{13,11},{18,20},{1... | collective-permute-start | bytes 860168 | tf_op jit(solution)/shard_map/ppermute | solution.py:86
  59.8 15.6 %collective-permute-start.13 = (bf16[80,1792]{1,0:T(8,128)(2,1)S(1)}, bf16[80,1792]{1,0:T(8,128)(2,1)S(1)}, u32[]{:S(2)}, u32[]{:S(2)}) collective-permute-start(bf16[80,1792]{1,0:T(8,128)(2,1)S(1)} %get-tuple-element.123), channel_id=1, source_target_pairs={{0,1},{1,0},{2,3},{3,2},{4,5},{5,4},{6,7},{7,6},{8,9},{9,8},{10,11... | collective-permute-start | bytes 860168 | tf_op jit(solution)/shard_map/ppermute | solution.py:82
  61.9 14.1 %collective-permute-start.14 = (bf16[80,1792]{1,0:T(8,128)(2,1)S(1)}, bf16[80,1792]{1,0:T(8,128)(2,1)S(1)}, u32[]{:S(2)}, u32[]{:S(2)}) collective-permute-start(bf16[80,1792]{1,0:T(8,128)(2,1)S(1)} %get-tuple-element.125.refs_4_), channel_id=1, source_target_pairs={{0,2},{1,3},{2,0},{3,1},{4,6},{5,7},{6,4},{7,5},{8,10},{9,11},{10,... | collective-permute-start | bytes 860168 | tf_op jit(solution)/shard_map/ppermute | solution.py:86
  71.0 5.1 %collective-permute-start.15 = (bf16[80,1792]{1,0:T(8,128)(2,1)S(1)}, bf16[80,1792]{1,0:T(8,128)(2,1)S(1)}, u32[]{:S(2)}, u32[]{:S(2)}) collective-permute-start(bf16[80,1792]{1,0:T(8,128)(2,1)S(1)} %get-tuple-element.126.refs_5_), channel_id=1, source_target_pairs={{2,4},{3,5},{4,2},{5,3},{10,12},{11,13},{12,10},{13,11},{18,20},{1... | collective-permute-start | bytes 860168 | tf_op jit(solution)/shard_map/ppermute | solution.py:86
  73.1 9.7 %collective-permute-start.22 = (bf16[80,1792]{1,0:T(8,128)(2,1)S(1)}, bf16[80,1792]{1,0:T(8,128)(2,1)S(1)}, u32[]{:S(2)}, u32[]{:S(2)}) collective-permute-start(bf16[80,1792]{1,0:T(8,128)(2,1)S(1)} %get-tuple-element.140.refs_4_), channel_id=1, source_target_pairs={{0,2},{1,3},{2,0},{3,1},{4,6},{5,7},{6,4},{7,5},{8,10},{9,11},{10,... | collective-permute-start | bytes 860168 | tf_op jit(solution)/shard_map/ppermute | solution.py:86
  74.7 8.8 %collective-permute-start.23 = (bf16[80,1792]{1,0:T(8,128)(2,1)S(1)}, bf16[80,1792]{1,0:T(8,128)(2,1)S(1)}, u32[]{:S(2)}, u32[]{:S(2)}) collective-permute-start(bf16[80,1792]{1,0:T(8,128)(2,1)S(1)} %get-tuple-element.141.refs_5_), channel_id=1, source_target_pairs={{2,4},{3,5},{4,2},{5,3},{10,12},{11,13},{12,10},{13,11},{18,20},{1... | collective-permute-start | bytes 860168 | tf_op jit(solution)/shard_map/ppermute | solution.py:86
  75.3 8.2 %collective-permute-start.21 = (bf16[80,1792]{1,0:T(8,128)(2,1)S(1)}, bf16[80,1792]{1,0:T(8,128)(2,1)S(1)}, u32[]{:S(2)}, u32[]{:S(2)}) collective-permute-start(bf16[80,1792]{1,0:T(8,128)(2,1)S(1)} %get-tuple-element.138), channel_id=1, source_target_pairs={{0,1},{1,0},{2,3},{3,2},{4,5},{5,4},{6,7},{7,6},{8,9},{9,8},{10,11... | collective-permute-start | bytes 860168 | tf_op jit(solution)/shard_map/ppermute | solution.py:82
  76.0 13.5 %collective-permute-start.12 = (bf16[80,1792]{1,0:T(8,128)(2,1)S(1)}, bf16[80,1792]{1,0:T(8,128)(2,1)S(1)}, u32[]{:S(2)}, u32[]{:S(2)}) collective-permute-start(bf16[80,1792]{1,0:T(8,128)(2,1)S(1)} %get-tuple-element.121), channel_id=1, source_target_pairs={{0,1},{1,0},{2,3},{3,2},{4,5},{5,4},{6,7},{7,6},{8,9},{9,8},{10,11... | collective-permute-start | bytes 860168 | tf_op jit(solution)/shard_map/ppermute | solution.py:82
  77.5 12.7 %collective-permute-start.19 = (bf16[80,1792]{1,0:T(8,128)(2,1)S(1)}, bf16[80,1792]{1,0:T(8,128)(2,1)S(1)}, u32[]{:S(2)}, u32[]{:S(2)}) collective-permute-start(bf16[80,1792]{1,0:T(8,128)(2,1)S(1)} %get-tuple-element.135.refs_4_), channel_id=1, source_target_pairs={{0,2},{1,3},{2,0},{3,1},{4,6},{5,7},{6,4},{7,5},{8,10},{9,11},{10,... | collective-permute-start | bytes 860168 | tf_op jit(solution)/shard_map/ppermute | solution.py:86
  82.8 7.4 %collective-permute-start.20 = (bf16[80,1792]{1,0:T(8,128)(2,1)S(1)}, bf16[80,1792]{1,0:T(8,128)(2,1)S(1)}, u32[]{:S(2)}, u32[]{:S(2)}) collective-permute-start(bf16[80,1792]{1,0:T(8,128)(2,1)S(1)} %get-tuple-element.136.refs_5_), channel_id=1, source_target_pairs={{2,4},{3,5},{4,2},{5,3},{10,12},{11,13},{12,10},{13,11},{18,20},{1... | collective-permute-start | bytes 860168 | tf_op jit(solution)/shard_map/ppermute | solution.py:86
  84.2 6.0 %collective-permute-start.24 = (bf16[80,1792]{1,0:T(8,128)(2,1)S(1)}, bf16[80,1792]{1,0:T(8,128)(2,1)S(1)}, u32[]{:S(2)}, u32[]{:S(2)}) collective-permute-start(bf16[80,1792]{1,0:T(8,128)(2,1)S(1)} %get-tuple-element.143.refs_2_), channel_id=1, source_target_pairs={{0,1},{1,0},{2,3},{3,2},{4,5},{5,4},{6,7},{7,6},{8,9},{9,8},{10,11... | collective-permute-start | bytes 860168 | tf_op jit(solution)/shard_map/ppermute | solution.py:82
  85.7 14.2 %collective-permute-start.27 = (bf16[80,1792]{1,0:T(8,128)(2,1)S(1)}, bf16[80,1792]{1,0:T(8,128)(2,1)S(1)}, u32[]{:S(2)}, u32[]{:S(2)}) collective-permute-start(bf16[80,1792]{1,0:T(8,128)(2,1)S(1)} %get-tuple-element.150.refs_2_), channel_id=1, source_target_pairs={{0,2},{1,3},{2,0},{3,1},{4,6},{5,7},{6,4},{7,5},{8,10},{9,11},{10,... | collective-permute-start | bytes 860168 | tf_op jit(solution)/shard_map/ppermute | solution.py:86
  89.5 14.3 %collective-permute-start.28 = (bf16[80,1792]{1,0:T(8,128)(2,1)S(1)}, bf16[80,1792]{1,0:T(8,128)(2,1)S(1)}, u32[]{:S(2)}, u32[]{:S(2)}) collective-permute-start(bf16[80,1792]{1,0:T(8,128)(2,1)S(1)} %get-tuple-element.151.refs_3_), channel_id=1, source_target_pairs={{2,4},{3,5},{4,2},{5,3},{10,12},{11,13},{12,10},{13,11},{18,20},{1... | collective-permute-start | bytes 860168 | tf_op jit(solution)/shard_map/ppermute | solution.py:86
  90.9 13.6 %collective-permute-start.29 = (bf16[80,1792]{1,0:T(8,128)(2,1)S(1)}, bf16[80,1792]{1,0:T(8,128)(2,1)S(1)}, u32[]{:S(2)}, u32[]{:S(2)}) collective-permute-start(bf16[80,1792]{1,0:T(8,128)(2,1)S(1)} %get-tuple-element.145.refs_2_), channel_id=1, source_target_pairs={{0,1},{1,0},{2,3},{3,2},{4,5},{5,4},{6,7},{7,6},{8,9},{9,8},{10,11... | collective-permute-start | bytes 860168 | tf_op jit(solution)/shard_map/ppermute | solution.py:82
  97.4 17.5 %collective-permute-start.36 = (bf16[320,1024]{1,0:T(8,128)(2,1)S(1)}, bf16[320,1024]{1,0:T(8,128)(2,1)S(1)}, u32[]{:S(2)}, u32[]{:S(2)}) collective-permute-start(bf16[320,1024]{1,0:T(8,128)(2,1)S(1)} %get-tuple-element.162.refs_0_), channel_id=1, source_target_pairs={{0,8},{8,0},{16,24},{24,16},{1,9},{9,1},{17,25},{25,17},{2,10},{10... | collective-permute-start | bytes 1966088 | tf_op jit(solution)/shard_map/ppermute | solution.py:459
  98.6 16.3 %collective-permute-start.37 = (bf16[320,1024]{1,0:T(8,128)(2,1)S(1)}, bf16[320,1024]{1,0:T(8,128)(2,1)S(1)}, u32[]{:S(2)}, u32[]{:S(2)}) collective-permute-start(bf16[320,1024]{1,0:T(8,128)(2,1)S(1)} %get-tuple-element.163.refs_2_), channel_id=1, source_target_pairs={{0,16},{8,24},{16,0},{24,8},{1,17},{9,25},{17,1},{25,9},{2,18},{10... | collective-permute-start | bytes 1966088 | tf_op jit(solution)/shard_map/ppermute | solution.py:459
  99.9 10.5 %collective-permute-start.25 = (bf16[80,1792]{1,0:T(8,128)(2,1)S(1)}, bf16[80,1792]{1,0:T(8,128)(2,1)S(1)}, u32[]{:S(2)}, u32[]{:S(2)}) collective-permute-start(bf16[80,1792]{1,0:T(8,128)(2,1)S(1)} %get-tuple-element.147.refs_2_), channel_id=1, source_target_pairs={{0,2},{1,3},{2,0},{3,1},{4,6},{5,7},{6,4},{7,5},{8,10},{9,11},{10,... | collective-permute-start | bytes 860168 | tf_op jit(solution)/shard_map/ppermute | solution.py:86
  103.8 7.7 %collective-permute-start.26 = (bf16[80,1792]{1,0:T(8,128)(2,1)S(1)}, bf16[80,1792]{1,0:T(8,128)(2,1)S(1)}, u32[]{:S(2)}, u32[]{:S(2)}) collective-permute-start(bf16[80,1792]{1,0:T(8,128)(2,1)S(1)} %get-tuple-element.148.refs_3_), channel_id=1, source_target_pairs={{2,4},{3,5},{4,2},{5,3},{10,12},{11,13},{12,10},{13,11},{18,20},{1... | collective-permute-start | bytes 860168 | tf_op jit(solution)/shard_map/ppermute | solution.py:86
  105.1 7.1 %collective-permute-start.30 = (bf16[80,1792]{1,0:T(8,128)(2,1)S(1)}, bf16[80,1792]{1,0:T(8,128)(2,1)S(1)}, u32[]{:S(2)}, u32[]{:S(2)}) collective-permute-start(bf16[80,1792]{1,0:T(8,128)(2,1)S(1)} %get-tuple-element.155.refs_3_), channel_id=1, source_target_pairs={{0,1},{1,0},{2,3},{3,2},{4,5},{5,4},{6,7},{7,6},{8,9},{9,8},{10,11... | collective-permute-start | bytes 860168 | tf_op jit(solution)/shard_map/ppermute | solution.py:82
  110.4 7.1 %collective-permute-start.33 = (bf16[80,1792]{1,0:T(8,128)(2,1)S(1)}, bf16[80,1792]{1,0:T(8,128)(2,1)S(1)}, u32[]{:S(2)}, u32[]{:S(2)}) collective-permute-start(bf16[80,1792]{1,0:T(8,128)(2,1)S(1)} %get-tuple-element.160.refs_2_), channel_id=1, source_target_pairs={{0,2},{1,3},{2,0},{3,1},{4,6},{5,7},{6,4},{7,5},{8,10},{9,11},{10,... | collective-permute-start | bytes 860168 | tf_op jit(solution)/shard_map/ppermute | solution.py:86
  111.6 8.9 %collective-permute-start.34 = (bf16[80,1792]{1,0:T(8,128)(2,1)S(1)}, bf16[80,1792]{1,0:T(8,128)(2,1)S(1)}, u32[]{:S(2)}, u32[]{:S(2)}) collective-permute-start(bf16[80,1792]{1,0:T(8,128)(2,1)S(1)} %get-tuple-element.161.refs_3_), channel_id=1, source_target_pairs={{2,4},{3,5},{4,2},{5,3},{10,12},{11,13},{12,10},{13,11},{18,20},{1... | collective-permute-start | bytes 860168 | tf_op jit(solution)/shard_map/ppermute | solution.py:86
  113.1 8.1 %collective-permute-start.35 = (bf16[80,1792]{1,0:T(8,128)(2,1)S(1)}, bf16[80,1792]{1,0:T(8,128)(2,1)S(1)}, u32[]{:S(2)}, u32[]{:S(2)}) collective-permute-start(bf16[80,1792]{1,0:T(8,128)(2,1)S(1)} %get-tuple-element.157.refs_3_), channel_id=1, source_target_pairs={{0,1},{1,0},{2,3},{3,2},{4,5},{5,4},{6,7},{7,6},{8,9},{9,8},{10,11... | collective-permute-start | bytes 860168 | tf_op jit(solution)/shard_map/ppermute | solution.py:82
  115.3 18.8 %collective-permute-start.42 = (bf16[320,1024]{1,0:T(8,128)(2,1)S(1)}, bf16[320,1024]{1,0:T(8,128)(2,1)S(1)}, u32[]{:S(2)}, u32[]{:S(2)}) collective-permute-start(bf16[320,1024]{1,0:T(8,128)(2,1)S(1)} %get-tuple-element.173.refs_0_), channel_id=1, source_target_pairs={{0,16},{8,24},{16,0},{24,8},{1,17},{9,25},{17,1},{25,9},{2,18},{10... | collective-permute-start | bytes 1966088 | tf_op jit(solution)/shard_map/ppermute | solution.py:459
  116.2 18.0 %collective-permute-start.43 = (bf16[320,1024]{1,0:T(8,128)(2,1)S(1)}, bf16[320,1024]{1,0:T(8,128)(2,1)S(1)}, u32[]{:S(2)}, u32[]{:S(2)}) collective-permute-start(bf16[320,1024]{1,0:T(8,128)(2,1)S(1)} %get-tuple-element.174.refs_2_), channel_id=1, source_target_pairs={{0,8},{8,0},{16,24},{24,16},{1,9},{9,1},{17,25},{25,17},{2,10},{10... | collective-permute-start | bytes 1966088 | tf_op jit(solution)/shard_map/ppermute | solution.py:459
  117.6 8.4 %collective-permute-start.31 = (bf16[80,1792]{1,0:T(8,128)(2,1)S(1)}, bf16[80,1792]{1,0:T(8,128)(2,1)S(1)}, u32[]{:S(2)}, u32[]{:S(2)}) collective-permute-start(bf16[80,1792]{1,0:T(8,128)(2,1)S(1)} %get-tuple-element.158.refs_2_), channel_id=1, source_target_pairs={{0,2},{1,3},{2,0},{3,1},{4,6},{5,7},{6,4},{7,5},{8,10},{9,11},{10,... | collective-permute-start | bytes 860168 | tf_op jit(solution)/shard_map/ppermute | solution.py:86
  120.5 8.4 %collective-permute-start.32 = (bf16[80,1792]{1,0:T(8,128)(2,1)S(1)}, bf16[80,1792]{1,0:T(8,128)(2,1)S(1)}, u32[]{:S(2)}, u32[]{:S(2)}) collective-permute-start(bf16[80,1792]{1,0:T(8,128)(2,1)S(1)} %get-tuple-element.159.refs_3_), channel_id=1, source_target_pairs={{2,4},{3,5},{4,2},{5,3},{10,12},{11,13},{12,10},{13,11},{18,20},{1... | collective-permute-start | bytes 860168 | tf_op jit(solution)/shard_map/ppermute | solution.py:86
  121.8 7.1 %collective-permute-start.38 = (bf16[80,1792]{1,0:T(8,128)(2,1)S(1)}, bf16[80,1792]{1,0:T(8,128)(2,1)S(1)}, u32[]{:S(2)}, u32[]{:S(2)}) collective-permute-start(bf16[80,1792]{1,0:T(8,128)(2,1)S(1)} %get-tuple-element.166.refs_4_), channel_id=1, source_target_pairs={{0,1},{1,0},{2,3},{3,2},{4,5},{5,4},{6,7},{7,6},{8,9},{9,8},{10,11... | collective-permute-start | bytes 860168 | tf_op jit(solution)/shard_map/ppermute | solution.py:82
  125.9 9.0 %collective-permute-start.40 = (bf16[80,1792]{1,0:T(8,128)(2,1)S(1)}, bf16[80,1792]{1,0:T(8,128)(2,1)S(1)}, u32[]{:S(2)}, u32[]{:S(2)}) collective-permute-start(bf16[80,1792]{1,0:T(8,128)(2,1)S(1)} %get-tuple-element.171.refs_2_), channel_id=1, source_target_pairs={{0,2},{1,3},{2,0},{3,1},{4,6},{5,7},{6,4},{7,5},{8,10},{9,11},{10,... | collective-permute-start | bytes 860168 | tf_op jit(solution)/shard_map/ppermute | solution.py:86
  129.5 5.4 %collective-permute-start.41 = (bf16[80,1792]{1,0:T(8,128)(2,1)S(1)}, bf16[80,1792]{1,0:T(8,128)(2,1)S(1)}, u32[]{:S(2)}, u32[]{:S(2)}) collective-permute-start(bf16[80,1792]{1,0:T(8,128)(2,1)S(1)} %get-tuple-element.168.refs_4_), channel_id=1, source_target_pairs={{0,1},{1,0},{2,3},{3,2},{4,5},{5,4},{6,7},{7,6},{8,9},{9,8},{10,11... | collective-permute-start | bytes 860168 | tf_op jit(solution)/shard_map/ppermute | solution.py:82
  130.7 10.8 %collective-permute-start.39 = (bf16[80,1792]{1,0:T(8,128)(2,1)S(1)}, bf16[80,1792]{1,0:T(8,128)(2,1)S(1)}, u32[]{:S(2)}, u32[]{:S(2)}) collective-permute-start(bf16[80,1792]{1,0:T(8,128)(2,1)S(1)} %get-tuple-element.169.refs_2_), channel_id=1, source_target_pairs={{0,2},{1,3},{2,0},{3,1},{4,6},{5,7},{6,4},{7,5},{8,10},{9,11},{10,... | collective-permute-start | bytes 860168 | tf_op jit(solution)/shard_map/ppermute | solution.py:86
  136.4 5.2 %collective-permute-start.44 = (bf16[80,1792]{1,0:T(8,128)(2,1)S(1)}, bf16[80,1792]{1,0:T(8,128)(2,1)S(1)}, u32[]{:S(2)}, u32[]{:S(2)}) collective-permute-start(bf16[80,1792]{1,0:T(8,128)(2,1)S(1)} %get-tuple-element.177.refs_5_), channel_id=1, source_target_pairs={{0,1},{1,0},{2,3},{3,2},{4,5},{5,4},{6,7},{7,6},{8,9},{9,8},{10,11... | collective-permute-start | bytes 860168 | tf_op jit(solution)/shard_map/ppermute | solution.py:82
  143.0 13.4 %collective-permute-start.45 = (bf16[80,1792]{1,0:T(8,128)(2,1)S(1)}, bf16[80,1792]{1,0:T(8,128)(2,1)S(1)}, u32[]{:S(2)}, u32[]{:S(2)}) collective-permute-start(bf16[80,1792]{1,0:T(8,128)(2,1)S(1)} %get-tuple-element.179.refs_5_), channel_id=1, source_target_pairs={{0,1},{1,0},{2,3},{3,2},{4,5},{5,4},{6,7},{7,6},{8,9},{9,8},{10,11... | collective-permute-start | bytes 860168 | tf_op jit(solution)/shard_map/ppermute | solution.py:82
Sparse Core Ops, SparseCore 0:
  10.3 41.5 all-gather.2

commit v2 on v0

--- a/solution.py
+++ b/solution.py
@@ -527,14 +527,14 @@
     advance(1)
     activate()
     advance(0)
-    advance(1)
+    advance(1, [act_rows])
     advance(0)
     acts.add(order)
     advance(1)
     advance(0)
+    advance(1)
+    advance(0)
     acts.add(order)
-    advance(1)
-    advance(0)
     advance(1)
     while acts.hop < len(acts.hops):
         acts.add(order)

time: 174 us -> 171 us (0.983)
  waiting for transfers between devices: 28.9 us -> 23.4 us
    ppermute x20, waiting for transfers between devices: 25.8 us -> 21.3 us  [move_chip(): lax.ppermute(x, 'mp', [(HALVES * a + c, HALVES * b + c) for a, b in pairs...]
  transfers between devices with their start and end apart: 47 -> 47, of which waited for: 9 -> 8; matrix products, arithmetic and copies ran while one was open for 0% -> 0% of each run, Pallas kernels for 33% -> 34%
where the time goes in v2:
time: 171 us
  Pallas kernels  72.4 us (42%)
  starting transfers between devices  58 us (34%)
  waiting for transfers between devices  23.4 us (14%)
  between operations  15 us (9%)
  local copies, waits for them, and re-layouts  1.73 us (1%)
    pallas_call x24, Pallas kernels, call(): pl.pallas_call(body, in_specs=in_specs + [anywhere] * len(tokens), out_sp...  72.4 us
    ppermute x20, starting transfers between devices, move_chip(): lax.ppermute(x, 'mp', [(HALVES * a + c, HALVES * b + c) for a, b in pairs...  33.9 us
    ppermute x20, waiting for transfers between devices, move_chip(): lax.ppermute(x, 'mp', [(HALVES * a + c, HALVES * b + c) for a, b in pairs...  21.3 us
    ppermute x16, starting transfers between devices, swap_core(): return lax.ppermute(x, 'mp', [(i, i ^ 1) for i in range(size)])  13.1 us
    ppermute x6, starting transfers between devices, swap_quarter(): return lax.ppermute(x, 'dp', [(i, i ^ step) for i in range(size)])  5.95 us
    ppermute x4, starting transfers between devices, send(): lax.ppermute(x, 'dp', [(i, i ^ step) for i in range(self.size)])  5.02 us
  transfers between devices with their start and end apart: 47, of which 8 were waited for; matrix products, arithmetic and copies ran while one was open for 0% of the time, Pallas kernels for 34%

profile of v2, /device:TPU:1, one launch (start us, length us, event | category | flops | bytes accessed | tf_op | source)
XLA Modules:
  0.0 170.7 jit_solution(15877428328256626404)
XLA Ops:
  7.2 2.9 %join_rows.1 = (bf16[80,3584]{1,0:T(8,128)(2,1)S(1)}, bf16[80,3584]{1,0:T(8,128)(2,1)S(1)}, bf16[80,2048]{1,0:T(8,128)(2,1)}, f32[8,128]{1,0:T(8,128)S(1)}) custom-call(bf16[128,3584]{1,0:T(8,128)(2,1)} %refs_0_.1, bf16[32,3584]{1,0:T(8,128)(2,1)} %refs_1_.4, bf16[64,2048]{1,0:T(8,128)(2,1)} %refs_2_.1, bf16[16,2048]{1,0:T(8,128)(2,1)} %refs_3_.2), custom_call_target="tpu_custom_call" | custom-call | tf_op jit(solution)/shard_map/join_rows/pallas_call | solution.py:58
  10.2 2.1 %collective-permute-start = (bf16[80,3584]{1,0:T(8,128)(2,1)S(1)}, bf16[80,3584]{1,0:T(8,128)(2,1)S(1)}, u32[]{:S(2)}, u32[]{:S(2)}) collective-permute-start(bf16[80,3584]{1,0:T(8,128)(2,1)S(1)} %get-tuple-element.95.refs_1_), channel_id=1, source_target_pairs={{0,16},{8,24},{16,0},{24,8},{1,17},{9,25},{17,1},{25,9},{2,18},{10... | collective-permute-start | bytes 1720328 | tf_op jit(solution)/shard_map/ppermute | solution.py:83
  12.3 1.2 collective-permute-start.2
  13.9 10.3 %load_and_multiply.1 = (bf16[80,1792]{1,0:T(8,128)(2,1)S(1)}, bf16[80,1792]{1,0:T(8,128)(2,1)S(1)}, bf16[80,1792]{1,0:T(8,128)(2,1)S(1)}, bf16[80,1792]{1,0:T(8,...) custom-call(s32[3]{0:T(128)S(1)} %pad_add_fusion.refs_0_, ...), custom_call_target="tpu_custom_call" | custom-call | tf_op jit(solution)/shard_map/load_and_multiply/pallas_call | solution.py:58
  24.2 1.6 collective-permute-start.5
  25.8 1.2 collective-permute-done.5.refs_2_
  27.0 1.4 line_step.14
  28.4 1.7 collective-permute-start.11
  30.1 1.4 line_step.15
  31.4 5.0 %multiply.3 = (bf16[80,1792]{1,0:T(8,128)(2,1)S(1)}, bf16[80,1792]{1,0:T(8,128)(2,1)S(1)}, bf16[80,1792]{1,0:T(8,128)(2,1)S(1)}, bf16[80,1792]{1,0:T(8,128)(2,1)S(1)}, f32[8,128]{1,0:T(8,128)S(1)}) custom-call(s32[3]{0:T(128)S(1)} %pad_add_fusion.refs_0_, bf16[80,3584]{1,0:T(8,128)(2,1)S(1)} %collective-permute-done.refs_1_, ...), custom_call_target="tpu_custom_call" | custom-call | tf_op jit(solution)/shard_map/multiply/pallas_call | solution.py:58
  36.4 1.0 collective-permute-start.10
  37.4 1.2 collective-permute-start.1
  38.6 1.1 collective-permute-start.3
  39.8 10.5 %collective-permute-done.11.refs_6_ = bf16[80,1792]{1,0:T(8,128)(2,1)S(1)} collective-permute-done((bf16[80,1792]{1,0:T(8,128)(2,1)S(1)}, bf16[80,1792]{1,0:T(8,128)(2,1)S(1)}, u32[]{:S(2)}, u32[]{:S(2)}) %collective-permute-start.11) | collective-permute-done | bytes 286752 | tf_op jit(solution)/shard_map/ppermute | solution.py:92
  50.6 1.6 line_step.16
  52.1 5.0 %multiply.4 = (bf16[80,1792]{1,0:T(8,128)(2,1)S(1)}, bf16[80,1792]{1,0:T(8,128)(2,1)S(1)}, bf16[80,1792]{1,0:T(8,128)(2,1)S(1)}, bf16[80,1792]{1,0:T(8,128)(2,1)S(1)}, f32[8,128]{1,0:T(8,128)S(1)}) custom-call(s32[3]{0:T(128)S(1)} %pad_add_fusion.refs_0_, bf16[80,3584]{1,0:T(8,128)(2,1)S(1)} %collective-permute-done.8.refs_1_.refs_4_, ...), custom_call_target="tpu_custom_call" | custom-call | tf_op jit(solution)/shard_map/multiply/pallas_call | solution.py:58
  57.4 1.0 collective-permute-done.7.refs_6_
  58.3 0.7 collective-permute-start.17
  59.1 0.7 collective-permute-start.18
  59.8 0.8 collective-permute-start.13
  60.6 1.4 line_step.17
  62.0 4.1 %collective-permute-start.14 = (bf16[80,1792]{1,0:T(8,128)(2,1)S(1)}, bf16[80,1792]{1,0:T(8,128)(2,1)S(1)}, u32[]{:S(2)}, u32[]{:S(2)}) collective-permute-start(bf16[80,1792]{1,0:T(8,128)(2,1)S(1)} %get-tuple-element.125.refs_4_), channel_id=1, source_target_pairs={{0,2},{1,3},{2,0},{3,1},{4,6},{5,7},{6,4},{7,5},{8,10},{9,11},{10,... | collective-permute-start | bytes 860168 | tf_op jit(solution)/shard_map/ppermute | solution.py:92
  66.1 0.7 collective-permute-start.15
  66.8 5.7 %multiply.5 = (bf16[80,1792]{1,0:T(8,128)(2,1)S(1)}, bf16[80,1792]{1,0:T(8,128)(2,1)S(1)}, bf16[80,1792]{1,0:T(8,128)(2,1)}, bf16[80,1792]{1,0:T(8,128)(2,1)}, f32[8,128]{1,0:T(8,128)S(1)}) custom-call(s32[3]{0:T(128)S(1)} %pad_add_fusion.refs_0_, bf16[80,3584]{1,0:T(8,128)(2,1)S(1)} %collective-permute-done.1.refs_1_.refs_4_, ...), custom_call_target="tpu_custom_call" | custom-call | tf_op jit(solution)/shard_map/multiply/pallas_call | solution.py:58
  72.5 1.4 line_step.18
  73.8 1.7 collective-permute-start.22
  75.5 0.7 collective-permute-start.23
  76.2 0.6 collective-permute-start.21
  77.0 1.4 line_step.19
  78.4 2.4 %collective-permute-start.19 = (bf16[80,1792]{1,0:T(8,128)(2,1)S(1)}, bf16[80,1792]{1,0:T(8,128)(2,1)S(1)}, u32[]{:S(2)}, u32[]{:S(2)}) collective-permute-start(bf16[80,1792]{1,0:T(8,128)(2,1)S(1)} %get-tuple-element.135.refs_4_), channel_id=1, source_target_pairs={{0,2},{1,3},{2,0},{3,1},{4,6},{5,7},{6,4},{7,5},{8,10},{9,11},{10,... | collective-permute-start | bytes 860168 | tf_op jit(solution)/shard_map/ppermute | solution.py:92
  80.8 6.1 %multiply_activations.1 = (bf16[320,1024]{1,0:T(8,128)(2,1)S(1)}, bf16[320,1024]{1,0:T(8,128)(2,1)S(1)}, f32[8,128]{1,0:T(8,128)S(1)}) custom-call(bf16[640,2048]{1,0:T(8,128)(2,1)} %all-gather.3.cloned.1.call-done.refs_0_.refs_8_, bf16[2048,1024]{1,0:T(8,128)(2,1)} %refs_1_.5, f32[8,128]{1,0:T(8,128)S(1)} %get-tuple-element.143.refs_2_), custom_call_target="tpu_custom_call" | custom-call | tf_op jit(solution)/shard_map/multiply_activations/pallas_call | solution.py:58
  86.9 0.7 collective-permute-start.20
  87.6 1.1 line_step.20
  88.7 0.8 collective-permute-start.24
  89.4 1.2 collective-permute-start.31
  90.6 1.3 collective-permute-start.32
  91.9 1.7 %collective-permute-start.27 = (bf16[80,1792]{1,0:T(8,128)(2,1)S(1)}, bf16[80,1792]{1,0:T(8,128)(2,1)S(1)}, u32[]{:S(2)}, u32[]{:S(2)}) collective-permute-start(bf16[80,1792]{1,0:T(8,128)(2,1)S(1)} %get-tuple-element.152.refs_2_), channel_id=1, source_target_pairs={{0,2},{1,3},{2,0},{3,1},{4,6},{5,7},{6,4},{7,5},{8,10},{9,11},{10,... | collective-permute-start | bytes 860168 | tf_op jit(solution)/shard_map/ppermute | solution.py:92
  93.6 0.7 collective-permute-start.28
  94.3 1.7 %copy-done = bf16[640,2048]{1,0:T(8,128)(2,1)S(1)} copy-done((bf16[640,2048]{1,0:T(8,128)(2,1)S(1)}, bf16[640,2048]{1,0:T(8,128)(2,1)}, u32[]{:S(2)}) %copy-start) | copy-done | bytes 2621464
  96.1 0.7 line_step.21
  96.7 1.0 collective-permute-start.29
  97.7 2.5 %collective-permute-done.27.refs_4_ = bf16[80,1792]{1,0:T(8,128)(2,1)S(1)} collective-permute-done((bf16[80,1792]{1,0:T(8,128)(2,1)S(1)}, bf16[80,1792]{1,0:T(8,128)(2,1)S(1)}, u32[]{:S(2)}, u32[]{:S(2)}) %collective-permute-start.27) | collective-permute-done | bytes 286752 | tf_op jit(solution)/shard_map/ppermute | solution.py:92
  100.2 3.0 %collective-permute-start.25 = (bf16[80,1792]{1,0:T(8,128)(2,1)S(1)}, bf16[80,1792]{1,0:T(8,128)(2,1)S(1)}, u32[]{:S(2)}, u32[]{:S(2)}) collective-permute-start(bf16[80,1792]{1,0:T(8,128)(2,1)S(1)} %get-tuple-element.149.refs_2_), channel_id=1, source_target_pairs={{0,2},{1,3},{2,0},{3,1},{4,6},{5,7},{6,4},{7,5},{8,10},{9,11},{10,... | collective-permute-start | bytes 860168 | tf_op jit(solution)/shard_map/ppermute | solution.py:92
  103.2 0.7 collective-permute-start.26
  105.0 0.8 collective-permute-done.31.refs_1_
  105.8 5.5 %collective-permute-start.35 = (bf16[80,1792]{1,0:T(8,128)(2,1)S(1)}, bf16[80,1792]{1,0:T(8,128)(2,1)S(1)}, u32[]{:S(2)}, u32[]{:S(2)}) collective-permute-start(bf16[80,1792]{1,0:T(8,128)(2,1)S(1)} %get-tuple-element.163.refs_2_), channel_id=1, source_target_pairs={{0,2},{1,3},{2,0},{3,1},{4,6},{5,7},{6,4},{7,5},{8,10},{9,11},{10,... | collective-permute-start | bytes 860168 | tf_op jit(solution)/shard_map/ppermute | solution.py:92
  111.3 0.7 collective-permute-start.36
  112.3 0.8 line_step.23
  113.6 4.7 %collective-permute-start.33 = (bf16[80,1792]{1,0:T(8,128)(2,1)S(1)}, bf16[80,1792]{1,0:T(8,128)(2,1)S(1)}, u32[]{:S(2)}, u32[]{:S(2)}) collective-permute-start(bf16[80,1792]{1,0:T(8,128)(2,1)S(1)} %get-tuple-element.161.refs_2_), channel_id=1, source_target_pairs={{0,2},{1,3},{2,0},{3,1},{4,6},{5,7},{6,4},{7,5},{8,10},{9,11},{10,... | collective-permute-start | bytes 860168 | tf_op jit(solution)/shard_map/ppermute | solution.py:92
  118.3 0.7 collective-permute-start.34
  120.0 1.2 collective-permute-start.43
  121.2 1.4 collective-permute-start.44
  122.6 2.8 %collective-permute-done.33.refs_4_ = bf16[80,1792]{1,0:T(8,128)(2,1)S(1)} collective-permute-done((bf16[80,1792]{1,0:T(8,128)(2,1)S(1)}, bf16[80,1792]{1,0:T(8,128)(2,1)S(1)}, u32[]{:S(2)}, u32[]{:S(2)}) %collective-permute-start.33) | collective-permute-done | bytes 286752 | tf_op jit(solution)/shard_map/ppermute | solution.py:92
  125.4 1.3 collective-permute-start.40
  127.3 1.2 collective-permute-start.41
  128.5 1.7 %collective-permute-start.39 = (bf16[80,1792]{1,0:T(8,128)(2,1)S(1)}, bf16[80,1792]{1,0:T(8,128)(2,1)S(1)}, u32[]{:S(2)}, u32[]{:S(2)}) collective-permute-start(bf16[80,1792]{1,0:T(8,128)(2,1)S(1)} %get-tuple-element.169.refs_2_), channel_id=1, source_target_pairs={{0,2},{1,3},{2,0},{3,1},{4,6},{5,7},{6,4},{7,5},{8,10},{9,11},{10,... | collective-permute-start | bytes 860168 | tf_op jit(solution)/shard_map/ppermute | solution.py:92
  130.2 2.9 %collective-permute-done.40.refs_4_ = bf16[80,1792]{1,0:T(8,128)(2,1)S(1)} collective-permute-done((bf16[80,1792]{1,0:T(8,128)(2,1)S(1)}, bf16[80,1792]{1,0:T(8,128)(2,1)S(1)}, u32[]{:S(2)}, u32[]{:S(2)}) %collective-permute-start.40) | collective-permute-done | bytes 286752 | tf_op jit(solution)/shard_map/ppermute | solution.py:92
  133.1 1.4 line_step.26
  134.5 2.7 %collective-permute-start.42 = (bf16[80,1792]{1,0:T(8,128)(2,1)S(1)}, bf16[80,1792]{1,0:T(8,128)(2,1)S(1)}, u32[]{:S(2)}, u32[]{:S(2)}) collective-permute-start(bf16[80,1792]{1,0:T(8,128)(2,1)S(1)} %get-tuple-element.174.refs_5_), channel_id=1, source_target_pairs={{0,1},{1,0},{2,3},{3,2},{4,5},{5,4},{6,7},{7,6},{8,9},{9,8},{10,11... | collective-permute-start | bytes 860168 | tf_op jit(solution)/shard_map/ppermute | solution.py:88
  137.5 1.7 collective-permute-done.39.refs_4_
  139.2 1.4 line_step.27
  140.7 1.5 collective-permute-start.45
  142.8 10.5 %correct.2 = (f32[3584,1024]{1,0:T(8,128)}, bf16[4,3584,1024]{2,1,0:T(8,128)(2,1)}, f32[8,128]{1,0:T(8,128)S(1)}) custom-call(s32[3]{0:T(128)S(1)} %pad_add_fusion.refs_0_, f32[1]{0:T(128)S(6)} %copy.13.refs_1_, bf16[80,1792]{1,0:T(8,128)(2,1)S(1)} %get-tuple-element.145.refs_2_, bf16[80,1792]{1,0:T(8,128)(2,1)S(1)} %get-tuple-element.155.refs_3_, ...), custom_call_target="tpu_custom_call" | custom-call | tf_op jit(solution)/shard_map/correct/pallas_call | solution.py:58
  153.3 10.5 %correct.3 = (f32[3584,1024]{1,0:T(8,128)}, bf16[4,3584,1024]{2,1,0:T(8,128)(2,1)}, f32[8,128]{1,0:T(8,128)}) custom-call(s32[3]{0:T(128)S(1)} %pad_add_fusion.refs_0_, f32[1]{0:T(128)S(6)} %copy.13.refs_1_, bf16[80,1792]{1,0:T(8,128)(2,1)S(1)} %get-tuple-element.147.refs_2_, ...), custom_call_target="tpu_custom_call", output_to_operand_aliasing={{0}: (12, {}), {1}: (13, {})} | custom-call | tf_op jit(solution)/shard_map/correct/pallas_call | solution.py:58
  (58 shorter events, 5.0 us)
Async XLA Ops:
  7.2 73.6 %all-gather.3.cloned.1.call-start = ((), (), s32[]{:S(2)}) async-start(), calls=%async_computation | async-start | bytes 2949120 | tf_op jit(solution)/shard_map/all_gather | solution.py:461
  10.2 21.3 %collective-permute-start = (bf16[80,3584]{1,0:T(8,128)(2,1)S(1)}, bf16[80,3584]{1,0:T(8,128)(2,1)S(1)}, u32[]{:S(2)}, u32[]{:S(2)}) collective-permute-start(bf16[80,3584]{1,0:T(8,128)(2,1)S(1)} %get-tuple-element.95.refs_1_), channel_id=1, source_target_pairs={{0,16},{8,24},{16,0},{24,8},{1,17},{9,25},{17,1},{25,9},{2,18},{10... | collective-permute-start | bytes 1720328 | tf_op jit(solution)/shard_map/ppermute | solution.py:83
  12.3 19.1 %collective-permute-start.2 = (bf16[80,3584]{1,0:T(8,128)(2,1)S(1)}, bf16[80,3584]{1,0:T(8,128)(2,1)S(1)}, u32[]{:S(2)}, u32[]{:S(2)}) collective-permute-start(bf16[80,3584]{1,0:T(8,128)(2,1)S(1)} %get-tuple-element.96.refs_2_), channel_id=1, source_target_pairs={{0,8},{8,0},{16,24},{24,16},{1,9},{9,1},{17,25},{25,17},{2,10},{10... | collective-permute-start | bytes 1720328 | tf_op jit(solution)/shard_map/ppermute | solution.py:83
  13.5 25.1 %collective-permute-start.8 = (bf16[80,3584]{1,0:T(8,128)(2,1)S(1)}, bf16[80,3584]{1,0:T(8,128)(2,1)S(1)}, u32[]{:S(2)}, u32[]{:S(2)}) collective-permute-start(bf16[80,3584]{1,0:T(8,128)(2,1)S(1)} %get-tuple-element.95.refs_1_), channel_id=1, source_target_pairs={{0,8},{8,0},{16,24},{24,16},{1,9},{9,1},{17,25},{25,17},{2,10},{10... | collective-permute-start | bytes 1720328 | tf_op jit(solution)/shard_map/ppermute | solution.py:83
  24.2 2.8 %collective-permute-start.5 = (bf16[80,1792]{1,0:T(8,128)(2,1)S(1)}, bf16[80,1792]{1,0:T(8,128)(2,1)S(1)}, u32[]{:S(2)}, u32[]{:S(2)}) collective-permute-start(bf16[80,1792]{1,0:T(8,128)(2,1)S(1)} %get-tuple-element.102), channel_id=1, source_target_pairs={{0,1},{1,0},{2,3},{3,2},{4,5},{5,4},{6,7},{7,6},{8,9},{9,8},{10,11... | collective-permute-start | bytes 860168 | tf_op jit(solution)/shard_map/ppermute | solution.py:88
  25.7 2.7 %collective-permute-start.4 = (bf16[80,1792]{1,0:T(8,128)(2,1)S(1)}, bf16[80,1792]{1,0:T(8,128)(2,1)S(1)}, u32[]{:S(2)}, u32[]{:S(2)}) collective-permute-start(bf16[80,1792]{1,0:T(8,128)(2,1)S(1)} %get-tuple-element.100), channel_id=1, source_target_pairs={{0,1},{1,0},{2,3},{3,2},{4,5},{5,4},{6,7},{7,6},{8,9},{9,8},{10,11... | collective-permute-start | bytes 860168 | tf_op jit(solution)/shard_map/ppermute | solution.py:88
  27.0 25.1 %collective-permute-start.9 = (bf16[80,3584]{1,0:T(8,128)(2,1)S(1)}, bf16[80,3584]{1,0:T(8,128)(2,1)S(1)}, u32[]{:S(2)}, u32[]{:S(2)}) collective-permute-start(bf16[80,3584]{1,0:T(8,128)(2,1)S(1)} %get-tuple-element.96.refs_2_), channel_id=1, source_target_pairs={{0,16},{8,24},{16,0},{24,8},{1,17},{9,25},{17,1},{25,9},{2,18},{10... | collective-permute-start | bytes 1720328 | tf_op jit(solution)/shard_map/ppermute | solution.py:83
  28.4 21.8 %collective-permute-start.11 = (bf16[80,1792]{1,0:T(8,128)(2,1)S(1)}, bf16[80,1792]{1,0:T(8,128)(2,1)S(1)}, u32[]{:S(2)}, u32[]{:S(2)}) collective-permute-start(bf16[80,1792]{1,0:T(8,128)(2,1)S(1)} %get-tuple-element.114.refs_4_), channel_id=1, source_target_pairs={{0,2},{1,3},{2,0},{3,1},{4,6},{5,7},{6,4},{7,5},{8,10},{9,11},{10,... | collective-permute-start | bytes 860168 | tf_op jit(solution)/shard_map/ppermute | solution.py:92
  36.4 13.8 %collective-permute-start.10 = (bf16[80,1792]{1,0:T(8,128)(2,1)S(1)}, bf16[80,1792]{1,0:T(8,128)(2,1)S(1)}, u32[]{:S(2)}, u32[]{:S(2)}) collective-permute-start(bf16[80,1792]{1,0:T(8,128)(2,1)S(1)} %get-tuple-element.112), channel_id=1, source_target_pairs={{0,1},{1,0},{2,3},{3,2},{4,5},{5,4},{6,7},{7,6},{8,9},{9,8},{10,11... | collective-permute-start | bytes 860168 | tf_op jit(solution)/shard_map/ppermute | solution.py:88
  37.4 22.4 %collective-permute-start.1 = (bf16[80,3584]{1,0:T(8,128)(2,1)S(1)}, bf16[80,3584]{1,0:T(8,128)(2,1)S(1)}, u32[]{:S(2)}, u32[]{:S(2)}) collective-permute-start(bf16[80,3584]{1,0:T(8,128)(2,1)S(1)} %collective-permute-done.refs_1_), channel_id=1, source_target_pairs={{0,8},{8,0},{16,24},{24,16},{1,9},{9,1},{17,25},{25,17},{2,10},{10... | collective-permute-start | bytes 1720328 | tf_op jit(solution)/shard_map/ppermute | solution.py:83
  38.6 23.3 %collective-permute-start.3 = (bf16[80,3584]{1,0:T(8,128)(2,1)S(1)}, bf16[80,3584]{1,0:T(8,128)(2,1)S(1)}, u32[]{:S(2)}, u32[]{:S(2)}) collective-permute-start(bf16[80,3584]{1,0:T(8,128)(2,1)S(1)} %collective-permute-done.2.refs_2_), channel_id=1, source_target_pairs={{0,16},{8,24},{16,0},{24,8},{1,17},{9,25},{17,1},{25,9},{2,18},{10... | collective-permute-start | bytes 1720328 | tf_op jit(solution)/shard_map/ppermute | solution.py:83
  50.2 8.1 %collective-permute-start.7 = (bf16[80,1792]{1,0:T(8,128)(2,1)S(1)}, bf16[80,1792]{1,0:T(8,128)(2,1)S(1)}, u32[]{:S(2)}, u32[]{:S(2)}) collective-permute-start(bf16[80,1792]{1,0:T(8,128)(2,1)S(1)} %get-tuple-element.109.refs_4_), channel_id=1, source_target_pairs={{0,2},{1,3},{2,0},{3,1},{4,6},{5,7},{6,4},{7,5},{8,10},{9,11},{10,... | collective-permute-start | bytes 860168 | tf_op jit(solution)/shard_map/ppermute | solution.py:92
  50.2 8.8 %collective-permute-start.6 = (bf16[80,1792]{1,0:T(8,128)(2,1)S(1)}, bf16[80,1792]{1,0:T(8,128)(2,1)S(1)}, u32[]{:S(2)}, u32[]{:S(2)}) collective-permute-start(bf16[80,1792]{1,0:T(8,128)(2,1)S(1)} %get-tuple-element.107), channel_id=1, source_target_pairs={{0,1},{1,0},{2,3},{3,2},{4,5},{5,4},{6,7},{7,6},{8,9},{9,8},{10,11... | collective-permute-start | bytes 860168 | tf_op jit(solution)/shard_map/ppermute | solution.py:88
  57.1 9.0 %collective-permute-start.16 = (bf16[80,1792]{1,0:T(8,128)(2,1)S(1)}, bf16[80,1792]{1,0:T(8,128)(2,1)S(1)}, u32[]{:S(2)}, u32[]{:S(2)}) collective-permute-start(bf16[80,1792]{1,0:T(8,128)(2,1)S(1)} %get-tuple-element.128), channel_id=1, source_target_pairs={{0,1},{1,0},{2,3},{3,2},{4,5},{5,4},{6,7},{7,6},{8,9},{9,8},{10,11... | collective-permute-start | bytes 860168 | tf_op jit(solution)/shard_map/ppermute | solution.py:88
  58.3 14.1 %collective-permute-start.17 = (bf16[80,1792]{1,0:T(8,128)(2,1)S(1)}, bf16[80,1792]{1,0:T(8,128)(2,1)S(1)}, u32[]{:S(2)}, u32[]{:S(2)}) collective-permute-start(bf16[80,1792]{1,0:T(8,128)(2,1)S(1)} %get-tuple-element.130.refs_4_), channel_id=1, source_target_pairs={{0,2},{1,3},{2,0},{3,1},{4,6},{5,7},{6,4},{7,5},{8,10},{9,11},{10,... | collective-permute-start | bytes 860168 | tf_op jit(solution)/shard_map/ppermute | solution.py:92
  59.1 13.4 %collective-permute-start.18 = (bf16[80,1792]{1,0:T(8,128)(2,1)S(1)}, bf16[80,1792]{1,0:T(8,128)(2,1)S(1)}, u32[]{:S(2)}, u32[]{:S(2)}) collective-permute-start(bf16[80,1792]{1,0:T(8,128)(2,1)S(1)} %get-tuple-element.131.refs_5_), channel_id=1, source_target_pairs={{2,4},{3,5},{4,2},{5,3},{10,12},{11,13},{12,10},{13,11},{18,20},{1... | collective-permute-start | bytes 860168 | tf_op jit(solution)/shard_map/ppermute | solution.py:92
  59.8 16.4 %collective-permute-start.13 = (bf16[80,1792]{1,0:T(8,128)(2,1)S(1)}, bf16[80,1792]{1,0:T(8,128)(2,1)S(1)}, u32[]{:S(2)}, u32[]{:S(2)}) collective-permute-start(bf16[80,1792]{1,0:T(8,128)(2,1)S(1)} %get-tuple-element.123), channel_id=1, source_target_pairs={{0,1},{1,0},{2,3},{3,2},{4,5},{5,4},{6,7},{7,6},{8,9},{9,8},{10,11... | collective-permute-start | bytes 860168 | tf_op jit(solution)/shard_map/ppermute | solution.py:88
  62.0 14.9 %collective-permute-start.14 = (bf16[80,1792]{1,0:T(8,128)(2,1)S(1)}, bf16[80,1792]{1,0:T(8,128)(2,1)S(1)}, u32[]{:S(2)}, u32[]{:S(2)}) collective-permute-start(bf16[80,1792]{1,0:T(8,128)(2,1)S(1)} %get-tuple-element.125.refs_4_), channel_id=1, source_target_pairs={{0,2},{1,3},{2,0},{3,1},{4,6},{5,7},{6,4},{7,5},{8,10},{9,11},{10,... | collective-permute-start | bytes 860168 | tf_op jit(solution)/shard_map/ppermute | solution.py:92
  66.1 10.9 %collective-permute-start.15 = (bf16[80,1792]{1,0:T(8,128)(2,1)S(1)}, bf16[80,1792]{1,0:T(8,128)(2,1)S(1)}, u32[]{:S(2)}, u32[]{:S(2)}) collective-permute-start(bf16[80,1792]{1,0:T(8,128)(2,1)S(1)} %get-tuple-element.126.refs_5_), channel_id=1, source_target_pairs={{2,4},{3,5},{4,2},{5,3},{10,12},{11,13},{12,10},{13,11},{18,20},{1... | collective-permute-start | bytes 860168 | tf_op jit(solution)/shard_map/ppermute | solution.py:92
  73.8 13.0 %collective-permute-start.22 = (bf16[80,1792]{1,0:T(8,128)(2,1)S(1)}, bf16[80,1792]{1,0:T(8,128)(2,1)S(1)}, u32[]{:S(2)}, u32[]{:S(2)}) collective-permute-start(bf16[80,1792]{1,0:T(8,128)(2,1)S(1)} %get-tuple-element.141.refs_4_), channel_id=1, source_target_pairs={{0,2},{1,3},{2,0},{3,1},{4,6},{5,7},{6,4},{7,5},{8,10},{9,11},{10,... | collective-permute-start | bytes 860168 | tf_op jit(solution)/shard_map/ppermute | solution.py:92
  75.5 12.0 %collective-permute-start.23 = (bf16[80,1792]{1,0:T(8,128)(2,1)S(1)}, bf16[80,1792]{1,0:T(8,128)(2,1)S(1)}, u32[]{:S(2)}, u32[]{:S(2)}) collective-permute-start(bf16[80,1792]{1,0:T(8,128)(2,1)S(1)} %get-tuple-element.142.refs_5_), channel_id=1, source_target_pairs={{2,4},{3,5},{4,2},{5,3},{10,12},{11,13},{12,10},{13,11},{18,20},{1... | collective-permute-start | bytes 860168 | tf_op jit(solution)/shard_map/ppermute | solution.py:92
  76.2 11.3 %collective-permute-start.21 = (bf16[80,1792]{1,0:T(8,128)(2,1)}, bf16[80,1792]{1,0:T(8,128)(2,1)}, u32[]{:S(2)}, u32[]{:S(2)}) collective-permute-start(bf16[80,1792]{1,0:T(8,128)(2,1)} %get-tuple-element.139), channel_id=1, source_target_pairs={{0,1},{1,0},{2,3},{3,2},{4,5},{5,4},{6,7},{7,6},{8,9},{9,8},{10,11... | collective-permute-start | bytes 860168 | tf_op jit(solution)/shard_map/ppermute | solution.py:88
  76.9 13.8 %collective-permute-start.12 = (bf16[80,1792]{1,0:T(8,128)(2,1)}, bf16[80,1792]{1,0:T(8,128)(2,1)S(1)}, u32[]{:S(2)}, u32[]{:S(2)}) collective-permute-start(bf16[80,1792]{1,0:T(8,128)(2,1)} %get-tuple-element.121), channel_id=1, source_target_pairs={{0,1},{1,0},{2,3},{3,2},{4,5},{5,4},{6,7},{7,6},{8,9},{9,8},{10,11... | collective-permute-start | bytes 860168 | tf_op jit(solution)/shard_map/ppermute | solution.py:88
  78.4 13.5 %collective-permute-start.19 = (bf16[80,1792]{1,0:T(8,128)(2,1)S(1)}, bf16[80,1792]{1,0:T(8,128)(2,1)S(1)}, u32[]{:S(2)}, u32[]{:S(2)}) collective-permute-start(bf16[80,1792]{1,0:T(8,128)(2,1)S(1)} %get-tuple-element.135.refs_4_), channel_id=1, source_target_pairs={{0,2},{1,3},{2,0},{3,1},{4,6},{5,7},{6,4},{7,5},{8,10},{9,11},{10,... | collective-permute-start | bytes 860168 | tf_op jit(solution)/shard_map/ppermute | solution.py:92
  86.9 6.8 %collective-permute-start.20 = (bf16[80,1792]{1,0:T(8,128)(2,1)S(1)}, bf16[80,1792]{1,0:T(8,128)(2,1)S(1)}, u32[]{:S(2)}, u32[]{:S(2)}) collective-permute-start(bf16[80,1792]{1,0:T(8,128)(2,1)S(1)} %get-tuple-element.136.refs_5_), channel_id=1, source_target_pairs={{2,4},{3,5},{4,2},{5,3},{10,12},{11,13},{12,10},{13,11},{18,20},{1... | collective-permute-start | bytes 860168 | tf_op jit(solution)/shard_map/ppermute | solution.py:92
  88.7 5.6 %collective-permute-start.24 = (bf16[80,1792]{1,0:T(8,128)(2,1)S(1)}, bf16[80,1792]{1,0:T(8,128)(2,1)S(1)}, u32[]{:S(2)}, u32[]{:S(2)}) collective-permute-start(bf16[80,1792]{1,0:T(8,128)(2,1)S(1)} %get-tuple-element.145.refs_2_), channel_id=1, source_target_pairs={{0,1},{1,0},{2,3},{3,2},{4,5},{5,4},{6,7},{7,6},{8,9},{9,8},{10,11... | collective-permute-start | bytes 860168 | tf_op jit(solution)/shard_map/ppermute | solution.py:88
  89.4 16.3 %collective-permute-start.31 = (bf16[320,1024]{1,0:T(8,128)(2,1)S(1)}, bf16[320,1024]{1,0:T(8,128)(2,1)S(1)}, u32[]{:S(2)}, u32[]{:S(2)}) collective-permute-start(bf16[320,1024]{1,0:T(8,128)(2,1)S(1)} %get-tuple-element.156.refs_0_), channel_id=1, source_target_pairs={{0,8},{8,0},{16,24},{24,16},{1,9},{9,1},{17,25},{25,17},{2,10},{10... | collective-permute-start | bytes 1966088 | tf_op jit(solution)/shard_map/ppermute | solution.py:449
  90.6 20.7 %collective-permute-start.32 = (bf16[320,1024]{1,0:T(8,128)(2,1)S(1)}, bf16[320,1024]{1,0:T(8,128)(2,1)S(1)}, u32[]{:S(2)}, u32[]{:S(2)}) collective-permute-start(bf16[320,1024]{1,0:T(8,128)(2,1)S(1)} %get-tuple-element.157.refs_2_), channel_id=1, source_target_pairs={{0,16},{8,24},{16,0},{24,8},{1,17},{9,25},{17,1},{25,9},{2,18},{10... | collective-permute-start | bytes 1966088 | tf_op jit(solution)/shard_map/ppermute | solution.py:449
  91.9 8.3 %collective-permute-start.27 = (bf16[80,1792]{1,0:T(8,128)(2,1)S(1)}, bf16[80,1792]{1,0:T(8,128)(2,1)S(1)}, u32[]{:S(2)}, u32[]{:S(2)}) collective-permute-start(bf16[80,1792]{1,0:T(8,128)(2,1)S(1)} %get-tuple-element.152.refs_2_), channel_id=1, source_target_pairs={{0,2},{1,3},{2,0},{3,1},{4,6},{5,7},{6,4},{7,5},{8,10},{9,11},{10,... | collective-permute-start | bytes 860168 | tf_op jit(solution)/shard_map/ppermute | solution.py:92
  93.6 9.6 %collective-permute-start.28 = (bf16[80,1792]{1,0:T(8,128)(2,1)S(1)}, bf16[80,1792]{1,0:T(8,128)(2,1)S(1)}, u32[]{:S(2)}, u32[]{:S(2)}) collective-permute-start(bf16[80,1792]{1,0:T(8,128)(2,1)S(1)} %get-tuple-element.153.refs_3_), channel_id=1, source_target_pairs={{2,4},{3,5},{4,2},{5,3},{10,12},{11,13},{12,10},{13,11},{18,20},{1... | collective-permute-start | bytes 860168 | tf_op jit(solution)/shard_map/ppermute | solution.py:92
  94.3 1.7 %copy-start = (bf16[640,2048]{1,0:T(8,128)(2,1)S(1)}, bf16[640,2048]{1,0:T(8,128)(2,1)}, u32[]{:S(2)}) copy-start(bf16[640,2048]{1,0:T(8,128)(2,1)} %all-gather.3.cloned.1.call-done.refs_0_.refs_8_) | copy-start | bytes 7864324
  96.7 7.2 %collective-permute-start.29 = (bf16[80,1792]{1,0:T(8,128)(2,1)S(1)}, bf16[80,1792]{1,0:T(8,128)(2,1)S(1)}, u32[]{:S(2)}, u32[]{:S(2)}) collective-permute-start(bf16[80,1792]{1,0:T(8,128)(2,1)S(1)} %get-tuple-element.147.refs_2_), channel_id=1, source_target_pairs={{0,1},{1,0},{2,3},{3,2},{4,5},{5,4},{6,7},{7,6},{8,9},{9,8},{10,11... | collective-permute-start | bytes 860168 | tf_op jit(solution)/shard_map/ppermute | solution.py:88
  100.2 12.1 %collective-permute-start.25 = (bf16[80,1792]{1,0:T(8,128)(2,1)S(1)}, bf16[80,1792]{1,0:T(8,128)(2,1)S(1)}, u32[]{:S(2)}, u32[]{:S(2)}) collective-permute-start(bf16[80,1792]{1,0:T(8,128)(2,1)S(1)} %get-tuple-element.149.refs_2_), channel_id=1, source_target_pairs={{0,2},{1,3},{2,0},{3,1},{4,6},{5,7},{6,4},{7,5},{8,10},{9,11},{10,... | collective-permute-start | bytes 860168 | tf_op jit(solution)/shard_map/ppermute | solution.py:92
  103.2 9.1 %collective-permute-start.26 = (bf16[80,1792]{1,0:T(8,128)(2,1)S(1)}, bf16[80,1792]{1,0:T(8,128)(2,1)S(1)}, u32[]{:S(2)}, u32[]{:S(2)}) collective-permute-start(bf16[80,1792]{1,0:T(8,128)(2,1)S(1)} %get-tuple-element.150.refs_3_), channel_id=1, source_target_pairs={{2,4},{3,5},{4,2},{5,3},{10,12},{11,13},{12,10},{13,11},{18,20},{1... | collective-permute-start | bytes 860168 | tf_op jit(solution)/shard_map/ppermute | solution.py:92
  104.5 7.8 %collective-permute-start.30 = (bf16[80,1792]{1,0:T(8,128)(2,1)S(1)}, bf16[80,1792]{1,0:T(8,128)(2,1)S(1)}, u32[]{:S(2)}, u32[]{:S(2)}) collective-permute-start(bf16[80,1792]{1,0:T(8,128)(2,1)S(1)} %get-tuple-element.155.refs_3_), channel_id=1, source_target_pairs={{0,1},{1,0},{2,3},{3,2},{4,5},{5,4},{6,7},{7,6},{8,9},{9,8},{10,11... | collective-permute-start | bytes 860168 | tf_op jit(solution)/shard_map/ppermute | solution.py:88
  105.8 13.2 %collective-permute-start.35 = (bf16[80,1792]{1,0:T(8,128)(2,1)S(1)}, bf16[80,1792]{1,0:T(8,128)(2,1)S(1)}, u32[]{:S(2)}, u32[]{:S(2)}) collective-permute-start(bf16[80,1792]{1,0:T(8,128)(2,1)S(1)} %get-tuple-element.163.refs_2_), channel_id=1, source_target_pairs={{0,2},{1,3},{2,0},{3,1},{4,6},{5,7},{6,4},{7,5},{8,10},{9,11},{10,... | collective-permute-start | bytes 860168 | tf_op jit(solution)/shard_map/ppermute | solution.py:92
  111.3 7.6 %collective-permute-start.36 = (bf16[80,1792]{1,0:T(8,128)(2,1)S(1)}, bf16[80,1792]{1,0:T(8,128)(2,1)S(1)}, u32[]{:S(2)}, u32[]{:S(2)}) collective-permute-start(bf16[80,1792]{1,0:T(8,128)(2,1)S(1)} %get-tuple-element.164.refs_3_), channel_id=1, source_target_pairs={{2,4},{3,5},{4,2},{5,3},{10,12},{11,13},{12,10},{13,11},{18,20},{1... | collective-permute-start | bytes 860168 | tf_op jit(solution)/shard_map/ppermute | solution.py:92
  113.2 5.8 %collective-permute-start.37 = (bf16[80,1792]{1,0:T(8,128)(2,1)S(1)}, bf16[80,1792]{1,0:T(8,128)(2,1)S(1)}, u32[]{:S(2)}, u32[]{:S(2)}) collective-permute-start(bf16[80,1792]{1,0:T(8,128)(2,1)S(1)} %get-tuple-element.160.refs_3_), channel_id=1, source_target_pairs={{0,1},{1,0},{2,3},{3,2},{4,5},{5,4},{6,7},{7,6},{8,9},{9,8},{10,11... | collective-permute-start | bytes 860168 | tf_op jit(solution)/shard_map/ppermute | solution.py:88
  113.6 11.8 %collective-permute-start.33 = (bf16[80,1792]{1,0:T(8,128)(2,1)S(1)}, bf16[80,1792]{1,0:T(8,128)(2,1)S(1)}, u32[]{:S(2)}, u32[]{:S(2)}) collective-permute-start(bf16[80,1792]{1,0:T(8,128)(2,1)S(1)} %get-tuple-element.161.refs_2_), channel_id=1, source_target_pairs={{0,2},{1,3},{2,0},{3,1},{4,6},{5,7},{6,4},{7,5},{8,10},{9,11},{10,... | collective-permute-start | bytes 860168 | tf_op jit(solution)/shard_map/ppermute | solution.py:92
  118.3 8.4 %collective-permute-start.34 = (bf16[80,1792]{1,0:T(8,128)(2,1)S(1)}, bf16[80,1792]{1,0:T(8,128)(2,1)S(1)}, u32[]{:S(2)}, u32[]{:S(2)}) collective-permute-start(bf16[80,1792]{1,0:T(8,128)(2,1)S(1)} %get-tuple-element.162.refs_3_), channel_id=1, source_target_pairs={{2,4},{3,5},{4,2},{5,3},{10,12},{11,13},{12,10},{13,11},{18,20},{1... | collective-permute-start | bytes 860168 | tf_op jit(solution)/shard_map/ppermute | solution.py:92
  119.6 7.1 %collective-permute-start.38 = (bf16[80,1792]{1,0:T(8,128)(2,1)S(1)}, bf16[80,1792]{1,0:T(8,128)(2,1)S(1)}, u32[]{:S(2)}, u32[]{:S(2)}) collective-permute-start(bf16[80,1792]{1,0:T(8,128)(2,1)S(1)} %get-tuple-element.166.refs_4_), channel_id=1, source_target_pairs={{0,1},{1,0},{2,3},{3,2},{4,5},{5,4},{6,7},{7,6},{8,9},{9,8},{10,11... | collective-permute-start | bytes 860168 | tf_op jit(solution)/shard_map/ppermute | solution.py:88
  120.0 17.2 %collective-permute-start.43 = (bf16[320,1024]{1,0:T(8,128)(2,1)S(1)}, bf16[320,1024]{1,0:T(8,128)(2,1)S(1)}, u32[]{:S(2)}, u32[]{:S(2)}) collective-permute-start(bf16[320,1024]{1,0:T(8,128)(2,1)S(1)} %get-tuple-element.175.refs_0_), channel_id=1, source_target_pairs={{0,16},{8,24},{16,0},{24,8},{1,17},{9,25},{17,1},{25,9},{2,18},{10... | collective-permute-start | bytes 1966088 | tf_op jit(solution)/shard_map/ppermute | solution.py:449
  121.2 16.0 %collective-permute-start.44 = (bf16[320,1024]{1,0:T(8,128)(2,1)S(1)}, bf16[320,1024]{1,0:T(8,128)(2,1)S(1)}, u32[]{:S(2)}, u32[]{:S(2)}) collective-permute-start(bf16[320,1024]{1,0:T(8,128)(2,1)S(1)} %get-tuple-element.176.refs_2_), channel_id=1, source_target_pairs={{0,8},{8,0},{16,24},{24,16},{1,9},{9,1},{17,25},{25,17},{2,10},{10... | collective-permute-start | bytes 1966088 | tf_op jit(solution)/shard_map/ppermute | solution.py:449
  125.4 7.7 %collective-permute-start.40 = (bf16[80,1792]{1,0:T(8,128)(2,1)S(1)}, bf16[80,1792]{1,0:T(8,128)(2,1)S(1)}, u32[]{:S(2)}, u32[]{:S(2)}) collective-permute-start(bf16[80,1792]{1,0:T(8,128)(2,1)S(1)} %get-tuple-element.171.refs_2_), channel_id=1, source_target_pairs={{0,2},{1,3},{2,0},{3,1},{4,6},{5,7},{6,4},{7,5},{8,10},{9,11},{10,... | collective-permute-start | bytes 860168 | tf_op jit(solution)/shard_map/ppermute | solution.py:92
  127.3 5.8 %collective-permute-start.41 = (bf16[80,1792]{1,0:T(8,128)(2,1)S(1)}, bf16[80,1792]{1,0:T(8,128)(2,1)S(1)}, u32[]{:S(2)}, u32[]{:S(2)}) collective-permute-start(bf16[80,1792]{1,0:T(8,128)(2,1)S(1)} %get-tuple-element.168.refs_4_), channel_id=1, source_target_pairs={{0,1},{1,0},{2,3},{3,2},{4,5},{5,4},{6,7},{7,6},{8,9},{9,8},{10,11... | collective-permute-start | bytes 860168 | tf_op jit(solution)/shard_map/ppermute | solution.py:88
  128.5 10.7 %collective-permute-start.39 = (bf16[80,1792]{1,0:T(8,128)(2,1)S(1)}, bf16[80,1792]{1,0:T(8,128)(2,1)S(1)}, u32[]{:S(2)}, u32[]{:S(2)}) collective-permute-start(bf16[80,1792]{1,0:T(8,128)(2,1)S(1)} %get-tuple-element.169.refs_2_), channel_id=1, source_target_pairs={{0,2},{1,3},{2,0},{3,1},{4,6},{5,7},{6,4},{7,5},{8,10},{9,11},{10,... | collective-permute-start | bytes 860168 | tf_op jit(solution)/shard_map/ppermute | solution.py:92
  134.5 4.7 %collective-permute-start.42 = (bf16[80,1792]{1,0:T(8,128)(2,1)S(1)}, bf16[80,1792]{1,0:T(8,128)(2,1)S(1)}, u32[]{:S(2)}, u32[]{:S(2)}) collective-permute-start(bf16[80,1792]{1,0:T(8,128)(2,1)S(1)} %get-tuple-element.174.refs_5_), channel_id=1, source_target_pairs={{0,1},{1,0},{2,3},{3,2},{4,5},{5,4},{6,7},{7,6},{8,9},{9,8},{10,11... | collective-permute-start | bytes 860168 | tf_op jit(solution)/shard_map/ppermute | solution.py:88
  140.7 12.7 %collective-permute-start.45 = (bf16[80,1792]{1,0:T(8,128)(2,1)S(1)}, bf16[80,1792]{1,0:T(8,128)(2,1)S(1)}, u32[]{:S(2)}, u32[]{:S(2)}) collective-permute-start(bf16[80,1792]{1,0:T(8,128)(2,1)S(1)} %get-tuple-element.179.refs_5_), channel_id=1, source_target_pairs={{0,1},{1,0},{2,3},{3,2},{4,5},{5,4},{6,7},{7,6},{8,9},{9,8},{10,11... | collective-permute-start | bytes 860168 | tf_op jit(solution)/shard_map/ppermute | solution.py:88
Sparse Core Ops, SparseCore 0:
  10.3 41.7 all-gather.2
